TPU v7x, 128 devices: a whole 4x4x4 slice. The times are simulated.
128 devices in a mesh: deg: 16 (over y, x), ord: 8 (over z, core).
Axes of the slice: x: 4, y: 4, z: 4, core: 2. Of those that a mesh axis runs over, the one named last changes fastest.
Arguments:
- coefficients: bfloat16 [2048, 2048, 128], P('ord', 'deg'), as said below
- legendre: bfloat16 [2048, 2048, 256], P('ord', 'deg'), as said below
- order_table: int32 [2048], replicated, may hold values from 0 to 2047, as said below
Outputs:
- products: bfloat16 [256, 32, 4096], P(('deg', 'ord'))
Inputs may be any that keep to these rules, and one draw needn't show every extreme that they name: `order_table`: every order from 0 to 2047 appears once. For each index j of ord, with H = 128, the slots j * 256 to j * 256 + H - 1 hold orders below 1024, and slot j * 256 + H + s holds 2047 minus the order of slot j * 256 + s. `legendre`: zero at every degree below the order of its slot. `coefficients`: zero at every degree below the order of its slot.
All inputs are finite; a program needn't handle non-finite values.
Results may differ from a plain program's by a relative error of at most 0.025.
Values may be sent and summed in bfloat16 or wider, within the bound.
No kernel may reach another device: no remote copies, remote signals or barrier semaphores. Data moves between devices by JAX's collectives and lax.ppermute only.
A program may use at most 128 MiB of HBM per device.

v0:
```python
import math

import jax
import jax.numpy as jnp
from jax import lax
from jax.sharding import PartitionSpec as P

NLON = 4096


def build_tables(order_table, weight, index, block, nlon):
    fine = 64
    coarse = block // fine
    outer = lax.iota(jnp.int32, coarse) + index * coarse
    inner = lax.iota(jnp.int32, fine)
    factor = 2.0 * math.pi / nlon
    big_angle = (order_table[:, None] * (outer[None, :] * fine) % nlon).astype(jnp.float32) * factor
    small_angle = (order_table[:, None] * inner[None, :] % nlon).astype(jnp.float32) * factor
    cos_big = jnp.cos(big_angle)[:, :, None]
    sin_big = jnp.sin(big_angle)[:, :, None]
    cos_small = jnp.cos(small_angle)[:, None, :]
    sin_small = jnp.sin(small_angle)[:, None, :]
    scaled = weight[:, None, None]
    cos_full = scaled * (cos_big * cos_small - sin_big * sin_small)
    sin_full = -(scaled * (sin_big * cos_small + cos_big * sin_small))
    count = order_table.shape[0]
    return (
        cos_full.reshape(count, block).astype(jnp.bfloat16),
        sin_full.reshape(count, block).astype(jnp.bfloat16),
    )


def local(coefficients, legendre, order_table):
    channels = coefficients.shape[2]
    nfield = channels // 2
    partial_sum = jnp.einsum(
        "slt,slc->tsc", legendre, coefficients, preferred_element_type=jnp.float32
    )
    summed = lax.psum_scatter(
        partial_sum.astype(jnp.bfloat16).astype(jnp.float32).astype(jnp.bfloat16),
        "deg",
        scatter_dimension=0,
        tiled=True,
    )
    spectra = lax.all_to_all(summed, "ord", split_axis=0, concat_axis=1, tiled=True)
    rows_here = spectra.shape[0]
    spec_real = spectra[:, :, :nfield]
    spec_imag = spectra[:, :, nfield:]
    weight = jnp.where(order_table == 0, 1.0, 2.0).astype(jnp.float32)
    block = min(1024, NLON)
    count = NLON // block

    def one_block(index):
        cos_table, sin_table = build_tables(order_table, weight, index, block, NLON)
        grid = jnp.einsum("kmf,mn->kfn", spec_real, cos_table, preferred_element_type=jnp.float32)
        grid = grid + jnp.einsum(
            "kmf,mn->kfn", spec_imag, sin_table, preferred_element_type=jnp.float32
        )
        return grid[:, 0::2, :] * grid[:, 1::2, :]

    blocks = lax.map(one_block, jnp.arange(count, dtype=jnp.int32))
    result = jnp.transpose(blocks, (1, 2, 0, 3)).reshape(rows_here, nfield // 2, NLON)
    return result.astype(jnp.bfloat16)


def solution(mesh):
    placed = (P("ord", "deg", None), P("ord", "deg", None), P())
    return jax.shard_map(
        local, mesh=mesh, in_specs=placed, out_specs=P(("deg", "ord"), None, None), check_vma=False
    )
```

profile of v0, /device:TPU:1, one launch (start us, length us, event | category | flops | bytes accessed | tf_op | source)
XLA Modules:
  0.0 308.4 jit_solution(4508725382496535688)
XLA Ops:
  6.5 16.6 %convert_bitcast_fusion = bf16[256,256,128]{0,2,1:T(8,128)(2,1)} fusion(bf16[256,128,128]{2,1,0:T(8,128)(2,1)} %param.5, bf16[256,128,256]{2,1,0:T(8,128)(2,1)} %param.6), kind=kOutput, calls=%fused_computation.31 | convolution fusion | flops 2155872256 | bytes 41943040 | tf_op jit(solution)/shard_map/slt,slc->tsc/dot_general | solution.py:36
  23.2 21.6 %copy.23 = bf16[256,256,128]{2,1,0:T(8,128)(2,1)} copy(bf16[256,256,128]{0,2,1:T(8,128)(2,1)} %convert_bitcast_fusion) | data formatting | bytes 33554432 | tf_op jit(solution)/shard_map/convert_element_type | solution.py:40
  44.8 113.4 %reduce-scatter.2.cloned.1.call-done = bf16[16,256,128]{2,1,0:T(8,128)(2,1)} async-done(((bf16[256,256,128]{2,1,0:T(8,128)(2,1)}), bf16[16,256,128]{2,1,0:T(8,128)(2,1)}) %reduce-scatter.2.cloned.1.call-update) | async-done | bytes 1048592 | tf_op jit(solution)/shard_map/reduce_scatter | solution.py:39
  158.3 5.6 %all-to-all-start = ((bf16[16,256,128]{2,1,0:T(8,128)(2,1)}), bf16[16,256,128]{2,1,0:T(8,128)(2,1)S(1)}, u32[]{:S(2)}, u32[]{:S(2)}) async-start(bf16[16,256,128]{2,1,0:T(8,128)(2,1)} %reduce-scatter.2.cloned.1.call-done), calls=%async_computation.1 | async-start | bytes 2097152 | tf_op jit(solution)/shard_map/all_to_all | solution.py:45
  163.8 15.1 %all-to-all-done = bf16[16,256,128]{2,1,0:T(8,128)(2,1)S(1)} async-done(((bf16[16,256,128]{2,1,0:T(8,128)(2,1)}), bf16[16,256,128]{2,1,0:T(8,128)(2,1)S(1)}, u32[]{:S(2)}, u32[]{:S(2)}) %all-to-all-start) | async-done | bytes 1048608 | tf_op jit(solution)/shard_map/all_to_all | solution.py:45
  180.1 120.7 %while.12 = (s32[]{:T(128)}, bf16[4,2,32,1024]{3,2,1,0:T(8,128)(2,1)S(1)}, f32[2048]{0:T(1024)S(1)}, s32[2048]{0:T(1024)S(1)}, s32[4]{0:T(128)S(1)}, /*index=5*/...) while((s32[]{:T(128)}, bf16[4,2,32,1024]{3,2,1,0:T(8,128)(2,1)S(1)}, ...), condition=%wide.region_2.3_spmd, body=%wide.region_1.2_spmd.sunk | while | flops 1099300864 | bytes 58482940 | solution.py:61
  182.0 2.0 fusion.38
  184.0 6.9 %multiply_add_fusion.2 = (f32[2048,16,64]{0,2,1:T(8,128)}, f32[2048,16,64]{0,2,1:T(8,128)}) fusion(f32[2048,64]{0,1:T(8,128)S(1)} %get-tuple-element.185, f32[2048,16]{0,1:T(8,128)S(1)} %get-tuple-element.186, f32[2048,64]{0,1:T(8,128)S(1)} %get-tuple-element.187, f32[2048,16]{0,1:T(8,128)S(1)} %get-tuple-element.188), kind=kLoop, calls=%fused_computation.5.clone.1 | loop fusion | flops 12582912 | bytes 18087936 | tf_op jit(solution)/shard_map/while/body/eval_jaxpr/add | solution.py:25
  190.9 11.5 %fusion.40 = (bf16[2048,1024]{0,1:T(8,128)(2,1)}, bf16[2048,1024]{0,1:T(8,128)(2,1)}) fusion(f32[2048,16,64]{0,2,1:T(8,128)} %get-tuple-element.189, f32[2048]{0:T(1024)S(1)} %get-tuple-element.213, f32[2048,16,64]{0,2,1:T(8,128)} %get-tuple-element.190), kind=kLoop, calls=%fused_computation.2.clone.1 | loop fusion | flops 10485760 | bytes 25174016 | tf_op jit(solution)/shard_map/while/body/eval_jaxpr/convert_element_type | solution.py:29
  202.4 3.7 %fusion.41 = f32[1024,128]{0,1:S(1)} fusion(bf16[2048,1024]{0,1:T(8,128)(2,1)} %get-tuple-element.191, bf16[2048,128]{0,1:T(8,128)(2,1)S(1)} %bitcast.66), kind=kOutput, calls=%fused_computation.35.clone.1 | convolution fusion | flops 536870912 | bytes 5242880 | tf_op jit(solution)/shard_map/while
  206.1 3.7 %fusion.42 = f32[1024,128]{0,1:S(1)} fusion(bf16[2048,1024]{0,1:T(8,128)(2,1)} %get-tuple-element.192, bf16[2048,128]{0,1:T(8,128)(2,1)S(1)} %bitcast.67), kind=kOutput, calls=%fused_computation.36.clone.1 | convolution fusion | flops 536870912 | bytes 5242880 | tf_op jit(solution)/shard_map/while
  214.2 6.9 %multiply_add_fusion.2 = (f32[2048,16,64]{0,2,1:T(8,128)}, f32[2048,16,64]{0,2,1:T(8,128)}) fusion(f32[2048,64]{0,1:T(8,128)S(1)} %get-tuple-element.185, f32[2048,16]{0,1:T(8,128)S(1)} %get-tuple-element.186, f32[2048,64]{0,1:T(8,128)S(1)} %get-tuple-element.187, f32[2048,16]{0,1:T(8,128)S(1)} %get-tuple-element.188), kind=kLoop, calls=%fused_computation.5.clone.1 | loop fusion | flops 12582912 | bytes 18087936 | tf_op jit(solution)/shard_map/while/body/eval_jaxpr/add | solution.py:25
  221.1 11.5 %fusion.40 = (bf16[2048,1024]{0,1:T(8,128)(2,1)}, bf16[2048,1024]{0,1:T(8,128)(2,1)}) fusion(f32[2048,16,64]{0,2,1:T(8,128)} %get-tuple-element.189, f32[2048]{0:T(1024)S(1)} %get-tuple-element.213, f32[2048,16,64]{0,2,1:T(8,128)} %get-tuple-element.190), kind=kLoop, calls=%fused_computation.2.clone.1 | loop fusion | flops 10485760 | bytes 25174016 | tf_op jit(solution)/shard_map/while/body/eval_jaxpr/convert_element_type | solution.py:29
  232.6 3.7 %fusion.41 = f32[1024,128]{0,1:S(1)} fusion(bf16[2048,1024]{0,1:T(8,128)(2,1)} %get-tuple-element.191, bf16[2048,128]{0,1:T(8,128)(2,1)S(1)} %bitcast.66), kind=kOutput, calls=%fused_computation.35.clone.1 | convolution fusion | flops 536870912 | bytes 5242880 | tf_op jit(solution)/shard_map/while
  236.3 3.7 %fusion.42 = f32[1024,128]{0,1:S(1)} fusion(bf16[2048,1024]{0,1:T(8,128)(2,1)} %get-tuple-element.192, bf16[2048,128]{0,1:T(8,128)(2,1)S(1)} %bitcast.67), kind=kOutput, calls=%fused_computation.36.clone.1 | convolution fusion | flops 536870912 | bytes 5242880 | tf_op jit(solution)/shard_map/while
  242.3 2.0 fusion.38
  244.3 6.9 %multiply_add_fusion.2 = (f32[2048,16,64]{0,2,1:T(8,128)}, f32[2048,16,64]{0,2,1:T(8,128)}) fusion(f32[2048,64]{0,1:T(8,128)S(1)} %get-tuple-element.185, f32[2048,16]{0,1:T(8,128)S(1)} %get-tuple-element.186, f32[2048,64]{0,1:T(8,128)S(1)} %get-tuple-element.187, f32[2048,16]{0,1:T(8,128)S(1)} %get-tuple-element.188), kind=kLoop, calls=%fused_computation.5.clone.1 | loop fusion | flops 12582912 | bytes 18087936 | tf_op jit(solution)/shard_map/while/body/eval_jaxpr/add | solution.py:25
  251.2 11.5 %fusion.40 = (bf16[2048,1024]{0,1:T(8,128)(2,1)}, bf16[2048,1024]{0,1:T(8,128)(2,1)}) fusion(f32[2048,16,64]{0,2,1:T(8,128)} %get-tuple-element.189, f32[2048]{0:T(1024)S(1)} %get-tuple-element.213, f32[2048,16,64]{0,2,1:T(8,128)} %get-tuple-element.190), kind=kLoop, calls=%fused_computation.2.clone.1 | loop fusion | flops 10485760 | bytes 25174016 | tf_op jit(solution)/shard_map/while/body/eval_jaxpr/convert_element_type | solution.py:29
  262.7 3.7 %fusion.41 = f32[1024,128]{0,1:S(1)} fusion(bf16[2048,1024]{0,1:T(8,128)(2,1)} %get-tuple-element.191, bf16[2048,128]{0,1:T(8,128)(2,1)S(1)} %bitcast.66), kind=kOutput, calls=%fused_computation.35.clone.1 | convolution fusion | flops 536870912 | bytes 5242880 | tf_op jit(solution)/shard_map/while
  266.4 3.7 %fusion.42 = f32[1024,128]{0,1:S(1)} fusion(bf16[2048,1024]{0,1:T(8,128)(2,1)} %get-tuple-element.192, bf16[2048,128]{0,1:T(8,128)(2,1)S(1)} %bitcast.67), kind=kOutput, calls=%fused_computation.36.clone.1 | convolution fusion | flops 536870912 | bytes 5242880 | tf_op jit(solution)/shard_map/while
  274.5 6.9 %multiply_add_fusion.2 = (f32[2048,16,64]{0,2,1:T(8,128)}, f32[2048,16,64]{0,2,1:T(8,128)}) fusion(f32[2048,64]{0,1:T(8,128)S(1)} %get-tuple-element.185, f32[2048,16]{0,1:T(8,128)S(1)} %get-tuple-element.186, f32[2048,64]{0,1:T(8,128)S(1)} %get-tuple-element.187, f32[2048,16]{0,1:T(8,128)S(1)} %get-tuple-element.188), kind=kLoop, calls=%fused_computation.5.clone.1 | loop fusion | flops 12582912 | bytes 18087936 | tf_op jit(solution)/shard_map/while/body/eval_jaxpr/add | solution.py:25
  281.4 11.5 %fusion.40 = (bf16[2048,1024]{0,1:T(8,128)(2,1)}, bf16[2048,1024]{0,1:T(8,128)(2,1)}) fusion(f32[2048,16,64]{0,2,1:T(8,128)} %get-tuple-element.189, f32[2048]{0:T(1024)S(1)} %get-tuple-element.213, f32[2048,16,64]{0,2,1:T(8,128)} %get-tuple-element.190), kind=kLoop, calls=%fused_computation.2.clone.1 | loop fusion | flops 10485760 | bytes 25174016 | tf_op jit(solution)/shard_map/while/body/eval_jaxpr/convert_element_type | solution.py:29
  292.9 3.7 %fusion.41 = f32[1024,128]{0,1:S(1)} fusion(bf16[2048,1024]{0,1:T(8,128)(2,1)} %get-tuple-element.191, bf16[2048,128]{0,1:T(8,128)(2,1)S(1)} %bitcast.66), kind=kOutput, calls=%fused_computation.35.clone.1 | convolution fusion | flops 536870912 | bytes 5242880 | tf_op jit(solution)/shard_map/while
  296.6 3.7 %fusion.42 = f32[1024,128]{0,1:S(1)} fusion(bf16[2048,1024]{0,1:T(8,128)(2,1)} %get-tuple-element.192, bf16[2048,128]{0,1:T(8,128)(2,1)S(1)} %bitcast.67), kind=kOutput, calls=%fused_computation.36.clone.1 | convolution fusion | flops 536870912 | bytes 5242880 | tf_op jit(solution)/shard_map/while
  (42 shorter events, 12.5 us)
Async XLA Ops:
  6.5 151.7 %reduce-scatter.2.cloned.1.call-start = ((), (), s32[]{:S(2)}) async-start(), calls=%async_computation.2 | async-start | bytes 17825792 | tf_op jit(solution)/shard_map/reduce_scatter | solution.py:39
  44.8 119.0 %copy-start = (s32[2048]{0:T(1024)S(1)}, s32[2048]{0:T(1024)}, u32[]{:S(2)}) copy-start(s32[2048]{0:T(1024)} %param.7) | copy-start | bytes 24580
  158.3 20.7 %all-to-all-start = ((bf16[16,256,128]{2,1,0:T(8,128)(2,1)}), bf16[16,256,128]{2,1,0:T(8,128)(2,1)S(1)}, u32[]{:S(2)}, u32[]{:S(2)}) async-start(bf16[16,256,128]{2,1,0:T(8,128)(2,1)} %reduce-scatter.2.cloned.1.call-done), calls=%async_computation.1 | async-start | bytes 2097152 | tf_op jit(solution)/shard_map/all_to_all | solution.py:45
Sparse Core Ops, SparseCore 0:
  45.0 113.2 reduce-scatter.1
where the time goes:
time: 309 us; the launch traced here: 308 us
  waiting for transfers between devices  129 us (42%)
  other arithmetic  84.5 us (27%)
  matrix products  46.2 us (15%)
  local copies, waits for them, and re-layouts  27.3 us (9%)
  between operations  13.4 us (4%)
  starting transfers between devices  5.56 us (2%)
    reduce_scatter x1, waiting for transfers between devices, local(): lax.psum_scatter(partial_sum.astype(jnp.bfloat16).astype(jnp.float32).ast...  113 us
    convert_element_type x4, other arithmetic, build_tables(): sin_full.reshape(count, block).astype(jnp.bfloat16)  46 us
    while x8, matrix products  29.6 us
    add x4, other arithmetic, build_tables(): sin_full = -(scaled * (sin_big * cos_small + cos_big * sin_small))  27.6 us
    convert_element_type x1, local copies, waits for them, and re-layouts, local(): partial_sum.astype(jnp.bfloat16).astype(jnp.float32).astype(jnp.bfloat16)  21.6 us
    dot_general x1, matrix products, local(): jnp.einsum('slt,slc->tsc', legendre, coefficients, preferred_element_type...  16.6 us
    all_to_all x1, waiting for transfers between devices, local(): lax.all_to_all(summed, 'ord', split_axis=0, concat_axis=1, tiled=True)  15.1 us
    cos x4, other arithmetic, build_tables(): cos_small = jnp.cos(small_angle)[:, None, :]  8.18 us
  transfers between devices with their start and end apart: 2, of which 2 were waited for; matrix products, arithmetic and copies ran while one was open for 0% of the time, Pallas kernels for 0%

commit v1 on v0

v1 whole, which is shorter than its diff:
```python
import math

import jax
import jax.numpy as jnp
from jax import lax
from jax.experimental import pallas as pl
from jax.experimental.pallas import tpu as pltpu
from jax.sharding import PartitionSpec as P

NLON = 4096
QUARTER = NLON // 4
WIDE = QUARTER + 256
F32 = jnp.float32
BF16 = jnp.bfloat16


def legendre_kernel(leg_ref, coef_ref, out_ref, turned):
    step = leg_ref.shape[0]
    for s in range(step):
        turned[:, s, :] = lax.dot_general(
            leg_ref[s], coef_ref[s], (((0,), (0,)), ((), ())), preferred_element_type=F32
        )
    out_ref[...] = turned[...].astype(BF16)


def legendre_sums(legendre, coefficients, step=16):
    slots, width, nlat = legendre.shape
    channels = coefficients.shape[2]
    return pl.pallas_call(
        legendre_kernel,
        out_shape=jax.ShapeDtypeStruct((nlat, slots, channels), BF16),
        grid=(slots // step,),
        in_specs=[
            pl.BlockSpec((step, width, nlat), lambda i: (i, 0, 0)),
            pl.BlockSpec((step, width, channels), lambda i: (i, 0, 0)),
        ],
        out_specs=pl.BlockSpec((nlat, step, channels), lambda i: (0, i, 0)),
        scratch_shapes=[pltpu.VMEM((nlat, step, channels), F32)],
        compiler_params=pltpu.CompilerParams(vmem_limit_bytes=40 * 2**20),
        name="legendre_sums",
    )(legendre, coefficients)


def table_kernel(cos_ref, sin_ref, cos_step, sin_step, cos_out, sin_out):
    c = cos_ref[...]
    s = sin_ref[...]
    dc = cos_step[...]
    ds = sin_step[...]
    for q in range(WIDE // 128):
        cos_out[:, pl.ds(128 * q, 128)] = c.astype(BF16)
        sin_out[:, pl.ds(128 * q, 128)] = (-s).astype(BF16)
        if q + 1 < WIDE // 128:
            c, s = c * dc - s * ds, s * dc + c * ds


def build_tables(order_table):
    count = order_table.shape[0]
    factor = 2.0 * math.pi / NLON
    weight = jnp.where(order_table == 0, 1.0, 2.0).astype(F32)[:, None]
    inner = lax.iota(jnp.int32, 128)
    small = (order_table[:, None] * inner[None, :] % NLON).astype(F32) * factor
    big = (order_table * 128 % NLON).astype(F32) * factor
    cos_big = jnp.broadcast_to(jnp.cos(big)[:, None], (count, 128))
    sin_big = jnp.broadcast_to(jnp.sin(big)[:, None], (count, 128))
    rows = 256
    narrow = pl.BlockSpec((rows, 128), lambda i: (i, 0))
    wide = pl.BlockSpec((rows, WIDE), lambda i: (i, 0))
    return pl.pallas_call(
        table_kernel,
        out_shape=[jax.ShapeDtypeStruct((count, WIDE), BF16)] * 2,
        grid=(count // rows,),
        in_specs=[narrow] * 4,
        out_specs=[wide] * 2,
        compiler_params=pltpu.CompilerParams(vmem_limit_bytes=40 * 2**20),
        name="build_tables",
    )(weight * jnp.cos(small), weight * jnp.sin(small), cos_big, sin_big)


def fourier_kernel(spec_ref, even_ref, pick_ref, turn_ref, cos_ref, sin_ref, out_ref,
                   left_cos, left_sin, plus, minus):
    blocks, lats, slots, channels = spec_ref.shape
    quart = channels // 4
    half = 2 * lats * quart
    step = pl.program_id(0)
    nsteps = pl.num_programs(0)

    @pl.when(step == 0)
    def _():
        for j in range(blocks):
            cols = pl.ds(j * slots, slots)
            even = even_ref[pl.ds(0, 1), cols]
            for k in range(lats):
                turned = lax.dot_general(
                    pick_ref[...], spec_ref[j, k], (((1,), (1,)), ((), ())),
                    preferred_element_type=F32,
                )
                evens = turned * even
                odds = turned - evens
                for o, part in enumerate((evens, odds)):
                    part = part.astype(BF16)
                    for h in range(2):
                        rows = pl.ds(o * half + (h * lats + k) * quart, quart)
                        left_cos[rows, cols] = part[h * quart:(h + 1) * quart]
                        left_sin[rows, cols] = part[(2 + h) * quart:(3 + h) * quart]

    cosines = jnp.dot(left_cos[...], cos_ref[...], preferred_element_type=F32)
    sines = jnp.dot(left_sin[...], sin_ref[...], preferred_element_type=F32)
    cos_sum = cosines[:half] + cosines[half:]
    cos_dif = cosines[:half] - cosines[half:]
    sin_sum = sines[:half] + sines[half:]
    sin_dif = sines[:half] - sines[half:]
    pairs = half // 2
    width = cos_ref.shape[1]
    cols = pl.ds(pl.multiple_of(step * width, width), width)

    def product(grid):
        return (grid[:pairs] * grid[pairs:]).astype(BF16)

    plus[:, cols] = product(cos_sum - sin_sum)
    minus[:, cols] = product(cos_dif - sin_dif)

    @pl.when(step < nsteps - 1)
    def _():
        first = product(cos_sum + sin_sum).reshape(lats, quart, width)
        third = product(cos_dif + sin_dif).reshape(lats, quart, width)
        out_ref[:, :, cols] = first
        out_ref[:, :, pl.ds(pl.multiple_of(2 * QUARTER + step * width, width), width)] = third

    @pl.when(step == nsteps - 1)
    def _():
        for b in range(QUARTER // 128):
            source = pl.ds(QUARTER - 128 - 128 * b, 256)
            for start, held in ((3 * QUARTER, plus), (QUARTER, minus)):
                block = jnp.dot(held[:, source], turn_ref[...], preferred_element_type=F32)
                out_ref[:, :, pl.ds(start + 128 * b, 128)] = block.astype(BF16).reshape(
                    lats, quart, 128
                )


def fourier_products(spectra, order_table, cos_table, sin_table):
    blocks, lats, slots, channels = spectra.shape
    count = order_table.shape[0]
    fields = channels // 2
    even = jnp.where(order_table % 2 == 0, 1.0, 0.0).astype(F32)
    even = jnp.broadcast_to(even[None, :], (8, count))
    c = lax.iota(jnp.int32, channels)
    part, field = c // fields, c % fields
    place = part * fields + (field % 2) * (fields // 2) + field // 2
    pick = (lax.iota(jnp.int32, channels)[:, None] == place[None, :]).astype(BF16)
    turn = (lax.iota(jnp.int32, 256)[:, None] == 128 - lax.iota(jnp.int32, 128)[None, :]).astype(BF16)
    width = 256
    full = lambda shape: pl.BlockSpec(shape, lambda i: (0,) * len(shape))
    half = lats * fields
    return pl.pallas_call(
        fourier_kernel,
        out_shape=jax.ShapeDtypeStruct((lats, fields // 2, NLON), BF16),
        grid=(WIDE // width,),
        in_specs=[
            full(spectra.shape),
            full(even.shape),
            full(pick.shape),
            full(turn.shape),
            pl.BlockSpec((count, width), lambda i: (0, i)),
            pl.BlockSpec((count, width), lambda i: (0, i)),
        ],
        out_specs=full((lats, fields // 2, NLON)),
        scratch_shapes=[
            pltpu.VMEM((2 * half, count), BF16),
            pltpu.VMEM((2 * half, count), BF16),
            pltpu.VMEM((half // 2, WIDE), BF16),
            pltpu.VMEM((half // 2, WIDE), BF16),
        ],
        compiler_params=pltpu.CompilerParams(vmem_limit_bytes=48 * 2**20),
        name="fourier_products",
    )(spectra, even, pick, turn, cos_table, sin_table)


def local(coefficients, legendre, order_table):
    partial = legendre_sums(legendre, coefficients)
    summed = lax.psum_scatter(partial, "deg", scatter_dimension=0, tiled=True)
    cos_table, sin_table = build_tables(order_table)
    rows, slots, channels = summed.shape
    groups = order_table.shape[0] // slots
    sent = summed.reshape(groups, rows // groups, slots, channels)
    spectra = lax.all_to_all(sent, "ord", split_axis=0, concat_axis=0, tiled=True)
    return fourier_products(spectra, order_table, cos_table, sin_table)


def solution(mesh):
    placed = (P("ord", "deg", None), P("ord", "deg", None), P())
    return jax.shard_map(
        local, mesh=mesh, in_specs=placed, out_specs=P(("deg", "ord"), None, None), check_vma=False
    )
```

time: 309 us -> 187 us (0.61)
  other arithmetic: 84.5 us -> 4.3 us
  matrix products: 46.2 us -> 0 us
  Pallas kernels: 0 us -> 40.9 us
  local copies, waits for them, and re-layouts: 27.3 us -> 7.05 us
  waiting for transfers between devices: 129 us -> 115 us
    convert_element_type x4 -> x2, other arithmetic: 46 us -> 0.03 us  [the longest x1 0.02 us: fourier_products(): (lax.iota(jnp.int32, 256)[:, None] == 128 - lax.iota(jnp.int32, 128)[None...]
    pallas_call x0 -> x3, Pallas kernels: none -> 40.9 us  [the longest x1 27 us: legendre_sums(): pl.pallas_call(legendre_kernel, out_shape=jax.ShapeDtypeStruct((nlat, slo...]
    while x8 -> x0, matrix products: 29.6 us -> none
    add x8 -> x1, other arithmetic: 27.8 us -> 0.01 us  [fourier_products(): place = part * fields + field % 2 * (fields // 2) + field // 2]
    convert_element_type x2 -> x0, local copies, waits for them, and re-layouts: 22.5 us -> none  [the longest x1 21.6 us: local(): partial_sum.astype(jnp.bfloat16).astype(jnp.float32).astype(jnp.bfloat16)]
    dot_general x1 -> x0, matrix products: 16.6 us -> none  [local(): jnp.einsum('slt,slc->tsc', legendre, coefficients, preferred_element_type...]
    all_to_all x1, waiting for transfers between devices: 15.1 us -> 2.49 us  [local(): lax.all_to_all(sent, 'ord', split_axis=0, concat_axis=0, tiled=True)]
    cos x8 -> x0, other arithmetic: 10.6 us -> none  [the longest x4 8.18 us: build_tables(): cos_small = jnp.cos(small_angle)[:, None, :]]
  transfers between devices with their start and end apart: 2 -> 2, of which waited for: 2 -> 2; matrix products, arithmetic and copies ran while one was open for 0% -> 3% of each run, Pallas kernels for 0% -> 3%
where the time goes in v1:
time: 187 us; the launch traced here: 186 us
  waiting for transfers between devices  115 us (61%)
  Pallas kernels  40.9 us (22%)
  between operations  13.4 us (7%)
  local copies, waits for them, and re-layouts  7.05 us (4%)
  starting transfers between devices  5.42 us (3%)
  other arithmetic  4.3 us (2%)
    reduce_scatter x1, waiting for transfers between devices, local(): summed = lax.psum_scatter(partial, 'deg', scatter_dimension=0, tiled=True)  113 us
    pallas_call x1, Pallas kernels, legendre_sums(): pl.pallas_call(legendre_kernel, out_shape=jax.ShapeDtypeStruct((nlat, slo...  27 us
    pallas_call x1, Pallas kernels, fourier_products(): pl.pallas_call(fourier_kernel, out_shape=jax.ShapeDtypeStruct((lats, fiel...  8.51 us
    unnamed x6, local copies, waits for them, and re-layouts  6.39 us
    all_to_all x1, starting transfers between devices, local(): lax.all_to_all(sent, 'ord', split_axis=0, concat_axis=0, tiled=True)  5.41 us
    pallas_call x1, Pallas kernels, build_tables(): pl.pallas_call(table_kernel, out_shape=[jax.ShapeDtypeStruct((count, WIDE...  5.33 us
    mul x1, other arithmetic, build_tables(): weight * jnp.sin(small)  4.19 us
  transfers between devices with their start and end apart: 2, of which 2 were waited for; matrix products, arithmetic and copies ran while one was open for 3% of the time, Pallas kernels for 3%

profile of v1, /device:TPU:1, one launch (start us, length us, event | category | flops | bytes accessed | tf_op | source)
XLA Modules:
  0.0 186.4 jit_solution(3887571982032556546)
XLA Ops:
  6.5 0.0 reduce-scatter.2.cloned.1.call-start
  6.5 0.0 copy-start
  6.5 3.4 %copy-done = bf16[256,128,128]{2,1,0:T(8,128)(2,1)S(1)} copy-done((bf16[256,128,128]{2,1,0:T(8,128)(2,1)S(1)}, bf16[256,128,128]{2,1,0:T(8,128)(2,1)}, u32[]{:S(2)}) %copy-start) | copy-done | bytes 8388632
  9.9 27.0 %legendre_sums.1 = bf16[256,256,128]{2,1,0:T(8,128)(2,1)} custom-call(bf16[256,128,256]{2,1,0:T(8,128)(2,1)} %leg_ref.1, bf16[256,128,128]{2,1,0:T(8,128)(2,1)S(1)} %copy-done), custom_call_target="tpu_custom_call" | custom-call | tf_op jit(solution)/shard_map/legendre_sums/pallas_call | solution.py:29
  36.9 0.0 copy-start.2
  36.9 0.0 reduce-scatter.2.cloned.1.call-update
  37.0 0.7 copy-done.2
  37.6 0.1 fusion.14
  37.7 112.8 %reduce-scatter.2.cloned.1.call-done = bf16[16,256,128]{2,1,0:T(8,128)(2,1)} async-done(((bf16[256,256,128]{2,1,0:T(8,128)(2,1)}), bf16[16,256,128]{2,1,0:T(8,128)(2,1)}) %reduce-scatter.2.cloned.1.call-update) | async-done | bytes 1048592 | tf_op jit(solution)/shard_map/reduce_scatter | solution.py:180
  150.5 5.4 %all-to-all-start = ((bf16[8,2,256,128]{3,2,1,0:T(8,128)(2,1)}), bf16[8,2,256,128]{3,2,1,0:T(8,128)(2,1)S(1)}, u32[]{:S(2)}, u32[]{:S(2)}) async-start(bf16[8,2,256,128]{3,2,1,0:T(8,128)(2,1)} %bitcast.1), calls=%async_computation.1 | async-start | bytes 2097152 | tf_op jit(solution)/shard_map/all_to_all | solution.py:185
  155.9 4.2 %sine_multiply_fusion = (f32[2048,128]{1,0:T(8,128)S(1)}, f32[2048,128]{1,0:T(8,128)S(1)}) fusion(s32[2048]{0:T(1024)S(1)} %copy-done.2, f32[2048]{0:T(1024)S(1)} %get-tuple-element.12), kind=kLoop, calls=%fused_computation.6 | loop fusion | flops 4194304 | bytes 2113536 | tf_op jit(solution)/shard_map/mul | solution.py:76
  160.1 0.3 broadcast_in_dim.22.cos_step
  160.5 0.3 broadcast_in_dim.42.sin_step
  160.8 5.3 %build_tables.1 = (bf16[2048,1280]{1,0:T(8,128)(2,1)S(1)}, bf16[2048,1280]{1,0:T(8,128)(2,1)}) custom-call(f32[2048,128]{1,0:T(8,128)S(1)} %get-tuple-element.10.cos_ref, f32[2048,128]{1,0:T(8,128)S(1)} %get-tuple-element.9.sin_ref, f32[2048,128]{1,0:T(8,128)S(1)} %broadcast_in_dim.22.cos_step, f32[2048,128]{1,0:T(8,128)S(1)} %broadcast_in_dim.42.sin_step), custom_call_target="tpu_custom_call" | custom-call | tf_op jit(solution)/shard_map/build_tables/pallas_call | solution.py:68
  166.1 0.0 copy-start.1
  166.1 2.3 %copy-done.1 = bf16[2048,1280]{1,0:T(8,128)(2,1)} copy-done((bf16[2048,1280]{1,0:T(8,128)(2,1)}, bf16[2048,1280]{1,0:T(8,128)(2,1)S(1)}, u32[]{:S(2)}) %copy-start.1) | copy-done | bytes 5242904
  168.5 2.5 %all-to-all-done.spec_ref = bf16[8,2,256,128]{3,2,1,0:T(8,128)(2,1)S(1)} async-done(((bf16[8,2,256,128]{3,2,1,0:T(8,128)(2,1)}), bf16[8,2,256,128]{3,2,1,0:T(8,128)(2,1)S(1)}, u32[]{:S(2)}, u32[]{:S(2)}) %all-to-all-start) | async-done | bytes 1048608 | tf_op jit(solution)/shard_map/all_to_all | solution.py:185
  171.0 8.5 %fourier_products.1 = bf16[2,32,4096]{2,1,0:T(8,128)(2,1)} custom-call(bf16[8,2,256,128]{3,2,1,0:T(8,128)(2,1)S(1)} %all-to-all-done.spec_ref, f32[8,2048]{1,0:T(8,128)S(1)} %broadcast_in_dim.20.even_ref, bf16[128,128]{1,0:T(8,128)(2,1)S(1)} %fusion.7.pick_ref, bf16[256,128]{1,0:T(8,128)(2,1)S(1)} %fusion.6.turn_ref, bf16[2048,1280]{1,0:T(8,128)(2,1)} %copy-done.1, ...), custom_call_target="tpu_custom_call" | custom-call | tf_op jit(solution)/shard_map/fourier_products/pallas_call | solution.py:154
  (5 shorter events, 0.1 us)
Async XLA Ops:
  6.5 144.0 %reduce-scatter.2.cloned.1.call-start = ((), (), s32[]{:S(2)}) async-start(), calls=%async_computation.2 | async-start | bytes 17825792 | tf_op jit(solution)/shard_map/reduce_scatter | solution.py:180
  6.5 3.4 %copy-start = (bf16[256,128,128]{2,1,0:T(8,128)(2,1)S(1)}, bf16[256,128,128]{2,1,0:T(8,128)(2,1)}, u32[]{:S(2)}) copy-start(bf16[256,128,128]{2,1,0:T(8,128)(2,1)} %coef_ref.1) | copy-start | bytes 25165828
  36.9 0.7 copy-start.2
  150.5 20.5 %all-to-all-start = ((bf16[8,2,256,128]{3,2,1,0:T(8,128)(2,1)}), bf16[8,2,256,128]{3,2,1,0:T(8,128)(2,1)S(1)}, u32[]{:S(2)}, u32[]{:S(2)}) async-start(bf16[8,2,256,128]{3,2,1,0:T(8,128)(2,1)} %bitcast.1), calls=%async_computation.1 | async-start | bytes 2097152 | tf_op jit(solution)/shard_map/all_to_all | solution.py:185
  166.1 2.3 %copy-start.1 = (bf16[2048,1280]{1,0:T(8,128)(2,1)}, bf16[2048,1280]{1,0:T(8,128)(2,1)S(1)}, u32[]{:S(2)}) copy-start(bf16[2048,1280]{1,0:T(8,128)(2,1)S(1)} %get-tuple-element.7.cos_ref) | copy-start | bytes 15728644
Sparse Core Ops, SparseCore 0:
  37.1 113.3 reduce-scatter.1

commit v2 on v1

--- a/solution.py
+++ b/solution.py
@@ -1,3 +1,4 @@
+import functools
 import math
 
 import jax
@@ -14,34 +15,152 @@
 BF16 = jnp.bfloat16
 
 
-def legendre_kernel(leg_ref, coef_ref, out_ref, turned):
+CHUNKS = 2
+SIDE = 4
+
+
+def legendre_kernel(place_ref, leg_ref, coef_ref, _, first_ref, second_ref, third_ref, one_ref,
+                    own_ref, turned, *, strides):
     step = leg_ref.shape[0]
-    for s in range(step):
-        turned[:, s, :] = lax.dot_general(
+    rows = turned.shape[0] // (SIDE * SIDE)
+    sums = [
+        lax.dot_general(
             leg_ref[s], coef_ref[s], (((0,), (0,)), ((), ())), preferred_element_type=F32
-        )
-    out_ref[...] = turned[...].astype(BF16)
-
-
-def legendre_sums(legendre, coefficients, step=16):
-    slots, width, nlat = legendre.shape
+        ).astype(BF16)
+        for s in range(step)
+    ]
+    turned[...] = jnp.swapaxes(jnp.stack(sums, axis=0), 0, 1)
+    here = (place_ref[0], place_ref[1])
+    half = SIDE // 2
+    parts = (
+        (first_ref, [(1, r) for r in range(half)] + [(2, r) for r in range(half)]),
+        (second_ref, [(3, r) for r in range(half, SIDE)] + [(2, r) for r in range(half, SIDE)]),
+        (third_ref, [(3, r) for r in range(half)]),
+        (one_ref, [(1, r) for r in range(half, SIDE)]),
+        (own_ref, [(0, r) for r in range(SIDE)]),
+    )
+    for ref, blocks in parts:
+        for i, (r1, r2) in enumerate(blocks):
+            block = (here[0] ^ r1) * strides[0] + (here[1] ^ r2) * strides[1]
+            source = pl.ds(pl.multiple_of(block * rows, rows), rows)
+            ref[i] = turned[source]
+
+
+def legendre_sums(place, legendre, coefficients, after, start, slots, strides, step=16):
+    width, nlat = legendre.shape[1:]
     channels = coefficients.shape[2]
+    rows = nlat // (SIDE * SIDE)
+    offset = start // step
+    counts = (4, 4, 2, 2, 4)
     return pl.pallas_call(
-        legendre_kernel,
-        out_shape=jax.ShapeDtypeStruct((nlat, slots, channels), BF16),
+        functools.partial(legendre_kernel, strides=strides),
+        out_shape=[jax.ShapeDtypeStruct((n, rows, slots, channels), BF16) for n in counts],
         grid=(slots // step,),
         in_specs=[
-            pl.BlockSpec((step, width, nlat), lambda i: (i, 0, 0)),
-            pl.BlockSpec((step, width, channels), lambda i: (i, 0, 0)),
+            pl.BlockSpec(memory_space=pltpu.SMEM),
+            pl.BlockSpec((step, width, nlat), lambda i: (i + offset, 0, 0)),
+            pl.BlockSpec((step, width, channels), lambda i: (i + offset, 0, 0)),
+            pl.BlockSpec(memory_space=pl.ANY),
         ],
-        out_specs=pl.BlockSpec((nlat, step, channels), lambda i: (0, i, 0)),
-        scratch_shapes=[pltpu.VMEM((nlat, step, channels), F32)],
+        out_specs=[pl.BlockSpec((n, rows, step, channels), lambda i: (0, 0, i, 0)) for n in counts],
+        scratch_shapes=[pltpu.VMEM((nlat, step, channels), BF16)],
         compiler_params=pltpu.CompilerParams(vmem_limit_bytes=40 * 2**20),
         name="legendre_sums",
-    )(legendre, coefficients)
-
-
-def table_kernel(cos_ref, sin_ref, cos_step, sin_step, cos_out, sin_out):
+    )(place, legendre, coefficients, after)
+
+
+def add(*parts):
+    total = parts[0].astype(F32)
+    for part in parts[1:]:
+        total = total + part.astype(F32)
+    return total.astype(BF16)
+
+
+def pass_kernel(got_first, got_second, third, one, first_out, second_out):
+    half = third.shape[0]
+    first_out[...] = add(third[...], got_first[half:])
+    second_out[...] = add(one[...], got_second[half:])
+
+
+def turn_kernel(*refs):
+    outs = refs[-5:]
+    first_out, second_out, third_out, one_out, own_out = outs
+    for c in range(CHUNKS):
+        got_first, got_second, last_first, last_second, own = refs[5 * c:5 * c + 5]
+        half = got_first.shape[0] // 2
+        rows, slots = own.shape[1] // 2, own.shape[2]
+        cols = pl.ds(c * slots, slots)
+
+        def sums(block, part):
+            if block < half:
+                got, last, at = got_first, last_first, block
+            else:
+                got, last, at = got_second, last_second, block - half
+            return add(own[block, part], got[at, part], last[at, part])
+
+        low, high = pl.ds(0, rows), pl.ds(rows, rows)
+        first_out[0:rows, cols] = sums(1, low)
+        first_out[rows:, cols] = sums(2, low)
+        second_out[0:rows, cols] = sums(3, high)
+        second_out[rows:, cols] = sums(2, high)
+        third_out[:, cols] = sums(3, low)
+        one_out[:, cols] = sums(1, high)
+        own_out[0:rows, cols] = sums(0, low)
+        own_out[rows:, cols] = sums(0, high)
+
+
+def join_kernel(*refs):
+    out = refs[-1]
+    count = (len(refs) - 1) // 5
+    slots = out.shape[1] // count
+    rows = out.shape[0] // 2
+    for i in range(count):
+        got_first, got_second, last_first, last_second, own = refs[5 * i:5 * i + 5]
+        cols = pl.ds(i * slots, slots)
+        out[0:rows, cols] = add(own[0:rows], got_first[0:rows], last_first[...])
+        out[rows:, cols] = add(own[rows:], got_second[0:rows], last_second[...])
+
+
+def call(kernel, name, shapes, after, *arrays):
+    return pl.pallas_call(
+        lambda _, *refs: kernel(*refs),
+        out_shape=[jax.ShapeDtypeStruct(s, BF16) for s in shapes],
+        in_specs=[pl.BlockSpec(memory_space=pl.ANY)]
+        + [pl.BlockSpec(memory_space=pltpu.VMEM)] * len(arrays),
+        compiler_params=pltpu.CompilerParams(vmem_limit_bytes=40 * 2**20),
+        name=name,
+    )(after, *arrays)
+
+
+def exchange(array, bits):
+    return lax.ppermute(array, "deg", [(d, d ^ bits) for d in range(SIDE * SIDE)])
+
+
+def start_sums(parts, unit):
+    first, second, third, one, own = parts
+    return exchange(first, unit), exchange(second, 3 * unit), third, one, own
+
+
+def pass_sums(state, unit, after):
+    got_first, got_second, third, one, own = state
+    send_first, send_second = call(
+        pass_kernel, "pass_sums", (third.shape, one.shape), after, got_first, got_second, third, one
+    )
+    last_first = exchange(send_first, 3 * unit)
+    last_second = exchange(send_second, unit)
+    return (got_first, got_second, last_first, last_second, own), send_second
+
+
+def turn_sums(states, unit, after):
+    rows, slots, channels = states[0][-1].shape[1:]
+    slots = slots * CHUNKS
+    whole, half = (rows, slots, channels), (rows // 2, slots, channels)
+    arrays = [a for state in states for a in state]
+    parts = call(turn_kernel, "turn_sums", (whole, whole, half, half, whole), after, *arrays)
+    return start_sums(parts, unit), parts[3]
+
+
+def table_kernel(_, cos_ref, sin_ref, cos_step, sin_step, cos_out, sin_out):
     c = cos_ref[...]
     s = sin_ref[...]
     dc = cos_step[...]
@@ -53,7 +172,7 @@
             c, s = c * dc - s * ds, s * dc + c * ds
 
 
-def build_tables(order_table):
+def build_tables(order_table, after):
     count = order_table.shape[0]
     factor = 2.0 * math.pi / NLON
     weight = jnp.where(order_table == 0, 1.0, 2.0).astype(F32)[:, None]
@@ -67,13 +186,13 @@
     wide = pl.BlockSpec((rows, WIDE), lambda i: (i, 0))
     return pl.pallas_call(
         table_kernel,
-        out_shape=[jax.ShapeDtypeStruct((count, WIDE), BF16)] * 2,
+        out_shape=[pltpu.HBM((count, WIDE), BF16)] * 2,
         grid=(count // rows,),
-        in_specs=[narrow] * 4,
+        in_specs=[pl.BlockSpec(memory_space=pl.ANY)] + [narrow] * 4,
         out_specs=[wide] * 2,
         compiler_params=pltpu.CompilerParams(vmem_limit_bytes=40 * 2**20),
         name="build_tables",
-    )(weight * jnp.cos(small), weight * jnp.sin(small), cos_big, sin_big)
+    )(after, weight * jnp.cos(small), weight * jnp.sin(small), cos_big, sin_big)
 
 
 def fourier_kernel(spec_ref, even_ref, pick_ref, turn_ref, cos_ref, sin_ref, out_ref,
@@ -170,20 +289,47 @@
             pltpu.VMEM((half // 2, WIDE), BF16),
             pltpu.VMEM((half // 2, WIDE), BF16),
         ],
-        compiler_params=pltpu.CompilerParams(vmem_limit_bytes=48 * 2**20),
+        compiler_params=pltpu.CompilerParams(vmem_limit_bytes=40 * 2**20),
         name="fourier_products",
     )(spectra, even, pick, turn, cos_table, sin_table)
 
 
 def local(coefficients, legendre, order_table):
-    partial = legendre_sums(legendre, coefficients)
-    summed = lax.psum_scatter(partial, "deg", scatter_dimension=0, tiled=True)
-    cos_table, sin_table = build_tables(order_table)
-    rows, slots, channels = summed.shape
-    groups = order_table.shape[0] // slots
-    sent = summed.reshape(groups, rows // groups, slots, channels)
+    here = lax.axis_index("deg")
+    y, x = here // SIDE, here % SIDE
+    total, channels = coefficients.shape[0], coefficients.shape[2]
+    groups = order_table.shape[0] // total
+    slots = total // (2 * CHUNKS)
+    coefficients = pltpu.with_memory_space_constraint(coefficients, pltpu.HBM)
+    legendre = pltpu.with_memory_space_constraint(legendre, pltpu.HBM)
+    units = ((1, SIDE), (SIDE, 1))
+    state = {}
+    after = order_table
+    keys = [(k, way) for k in range(CHUNKS) for way in range(2)]
+    for k, way in keys:
+        place = jnp.stack([x, y] if way == 0 else [y, x]).astype(jnp.int32)
+        parts = legendre_sums(
+            place, legendre, coefficients, after, (way * CHUNKS + k) * slots, slots, units[way]
+        )
+        after = parts[3]
+        state[k, way] = start_sums(parts, units[way][0])
+    tables = build_tables(order_table, after)
+    tables = [pltpu.with_memory_space_constraint(t, pltpu.HBM) for t in tables]
+    after = tables[0]
+    for k, way in keys:
+        state[k, way], after = pass_sums(state[k, way], units[way][0], after)
+    ends = []
+    for way in range(2):
+        end, after = turn_sums([state[k, way] for k in range(CHUNKS)], units[way][1], after)
+        ends.append(end)
+    for way in range(2):
+        ends[way], after = pass_sums(ends[way], units[way][1], after)
+    pair = ends[0] + ends[1]
+    rows = pair[-1].shape[0]
+    (summed,) = call(join_kernel, "join_sums", ((rows, total, channels),), after, *pair)
+    sent = summed.reshape(groups, rows // groups, total, channels)
     spectra = lax.all_to_all(sent, "ord", split_axis=0, concat_axis=0, tiled=True)
-    return fourier_products(spectra, order_table, cos_table, sin_table)
+    return fourier_products(spectra, order_table, *tables)
 
 
 def solution(mesh):

time: 187 us -> 155 us (0.83)
  waiting for transfers between devices: 115 us -> 60.1 us
  starting transfers between devices: 5.42 us -> 46.6 us
  between operations: 13.4 us -> 0.14 us
  local copies, waits for them, and re-layouts: 7.05 us -> 1.36 us
    reduce_scatter x1 -> x0, waiting for transfers between devices: 113 us -> none  [local(): summed = lax.psum_scatter(partial, 'deg', scatter_dimension=0, tiled=True)]
    ppermute x0 -> x24, waiting for transfers between devices: none -> 45 us  [exchange(): lax.ppermute(array, 'deg', [(d, d ^ bits) for d in range(SIDE * SIDE)])]
    ppermute x0 -> x24, starting transfers between devices: none -> 29.4 us  [exchange(): lax.ppermute(array, 'deg', [(d, d ^ bits) for d in range(SIDE * SIDE)])]
    all_to_all x1, waiting for transfers between devices: 2.49 us -> 15 us  [local(): lax.all_to_all(sent, 'ord', split_axis=0, concat_axis=0, tiled=True)]
    all_to_all x1, starting transfers between devices: 5.41 us -> 17.2 us  [local(): lax.all_to_all(sent, 'ord', split_axis=0, concat_axis=0, tiled=True)]
    unnamed x6 -> x2, local copies, waits for them, and re-layouts: 6.39 us -> 0.7 us
    pallas_call x2 -> x14, Pallas kernels: 32.4 us -> 33.9 us  [the longest x4 21.8 us: legendre_sums(): pl.pallas_call(functools.partial(legendre_kernel, strides=strides), out_s...]
  transfers between devices with their start and end apart: 2 -> 25, of which waited for: 2 -> 11; matrix products, arithmetic and copies ran while one was open for 3% -> 3% of each run, Pallas kernels for 3% -> 18%
where the time goes in v2:
time: 155 us
  waiting for transfers between devices  60.1 us (39%)
  starting transfers between devices  46.6 us (30%)
  Pallas kernels  42.5 us (27%)
  other arithmetic  4.38 us (3%)
    ppermute x24, waiting for transfers between devices, exchange(): lax.ppermute(array, 'deg', [(d, d ^ bits) for d in range(SIDE * SIDE)])  45 us
    ppermute x24, starting transfers between devices, exchange(): lax.ppermute(array, 'deg', [(d, d ^ bits) for d in range(SIDE * SIDE)])  29.4 us
    pallas_call x4, Pallas kernels, legendre_sums(): pl.pallas_call(functools.partial(legendre_kernel, strides=strides), out_s...  21.8 us
    all_to_all x1, starting transfers between devices, local(): lax.all_to_all(sent, 'ord', split_axis=0, concat_axis=0, tiled=True)  17.2 us
    all_to_all x1, waiting for transfers between devices, local(): lax.all_to_all(sent, 'ord', split_axis=0, concat_axis=0, tiled=True)  15 us
    pallas_call x1, Pallas kernels, fourier_products(): pl.pallas_call(fourier_kernel, out_shape=jax.ShapeDtypeStruct((lats, fiel...  8.51 us
    pallas_call x1, Pallas kernels, build_tables(): pl.pallas_call(table_kernel, out_shape=[pltpu.HBM((count, WIDE), BF16)] *...  6.68 us
    pallas_call x9, Pallas kernels, call(): pl.pallas_call(lambda _, *refs: kernel(*refs), out_shape=[jax.ShapeDtypeS...  5.51 us
  transfers between devices with their start and end apart: 25, of which 11 were waited for; matrix products, arithmetic and copies ran while one was open for 3% of the time, Pallas kernels for 18%

profile of v2, /device:TPU:1, one launch (start us, length us, event | category | flops | bytes accessed | tf_op | source)
XLA Modules:
  0.0 155.0 jit_solution(5345865134952937435)
XLA Ops:
  0.8 5.1 %legendre_sums.4 = (bf16[4,16,64,128]{3,2,1,0:T(8,128)(2,1)S(1)}, bf16[4,16,64,128]{3,2,1,0:T(8,128)(2,1)S(1)}, bf16[2,16,64,128]{3,2,1,0:T(8,128)(2,1)S(1)}, bf...) custom-call(s32[2]{0:T(128)S(1)} %get-tuple-element.100.place_ref, bf16[256,128,256]{2,1,0:T(8,128)(2,1)} %leg_ref.7, ...), custom_call_target="tpu_custom_call" | custom-call | tf_op jit(solution)/shard_map/legendre_sums/pallas_call | solution.py:55
  5.9 2.1 %collective-permute-start = (bf16[4,16,64,128]{3,2,1,0:T(8,128)(2,1)S(1)}, bf16[4,16,64,128]{3,2,1,0:T(8,128)(2,1)S(1)}, u32[]{:S(2)}, u32[]{:S(2)}) collective-permute-start(bf16[4,16,64,128]{3,2,1,0:T(8,128)(2,1)S(1)} %get-tuple-element.54), channel_id=1, source_target_pairs={{0,8},{8,0},{16,24},{24,16},{32,40},{40,32},{48,56},{56,48},{64,72... | collective-permute-start | bytes 3145736 | tf_op jit(solution)/shard_map/ppermute | solution.py:136
  9.9 5.7 %legendre_sums.5 = (bf16[4,16,64,128]{3,2,1,0:T(8,128)(2,1)S(1)}, bf16[4,16,64,128]{3,2,1,0:T(8,128)(2,1)}, bf16[2,16,64,128]{3,2,1,0:T(8,128)(2,1)S(1)}, bf16[2...) custom-call(s32[2]{0:T(128)S(1)} %get-tuple-element.99.place_ref, bf16[256,128,256]{2,1,0:T(8,128)(2,1)} %leg_ref.7, ...), custom_call_target="tpu_custom_call" | custom-call | tf_op jit(solution)/shard_map/legendre_sums/pallas_call | solution.py:55
  16.8 1.9 %collective-permute-start.3 = (bf16[4,16,64,128]{3,2,1,0:T(8,128)(2,1)}, bf16[4,16,64,128]{3,2,1,0:T(8,128)(2,1)S(1)}, u32[]{:S(2)}, u32[]{:S(2)}) collective-permute-start(bf16[4,16,64,128]{3,2,1,0:T(8,128)(2,1)} %get-tuple-element.59), channel_id=1, source_target_pairs={{0,96},{8,104},{16,112},{24,120},{32,64},{40,72},{48,80},{56,88},{... | collective-permute-start | bytes 3145736 | tf_op jit(solution)/shard_map/ppermute | solution.py:136
  18.7 5.8 %legendre_sums.6 = (bf16[4,16,64,128]{3,2,1,0:T(8,128)(2,1)}, bf16[4,16,64,128]{3,2,1,0:T(8,128)(2,1)}, bf16[2,16,64,128]{3,2,1,0:T(8,128)(2,1)S(1)}, bf16[2,16,...) custom-call(s32[2]{0:T(128)S(1)} %get-tuple-element.100.place_ref, bf16[256,128,256]{2,1,0:T(8,128)(2,1)} %leg_ref.7, ...), custom_call_target="tpu_custom_call" | custom-call | tf_op jit(solution)/shard_map/legendre_sums/pallas_call | solution.py:55
  24.8 5.6 %collective-permute-done.refs_0_ = bf16[4,16,64,128]{3,2,1,0:T(8,128)(2,1)S(1)} collective-permute-done((bf16[4,16,64,128]{3,2,1,0:T(8,128)(2,1)S(1)}, bf16[4,16,64,128]{3,2,1,0:T(8,128)(2,1)S(1)}, u32[]{:S(2)}, u32[]{:S(2)}) %collective-permute-start) | collective-permute-done | bytes 1048608 | tf_op jit(solution)/shard_map/ppermute | solution.py:136
  30.4 2.9 %collective-permute-start.5 = (bf16[4,16,64,128]{3,2,1,0:T(8,128)(2,1)}, bf16[4,16,64,128]{3,2,1,0:T(8,128)(2,1)S(1)}, u32[]{:S(2)}, u32[]{:S(2)}) collective-permute-start(bf16[4,16,64,128]{3,2,1,0:T(8,128)(2,1)} %get-tuple-element.63), channel_id=1, source_target_pairs={{0,24},{8,16},{16,8},{24,0},{32,56},{40,48},{48,40},{56,32},{64,88... | collective-permute-start | bytes 3145736 | tf_op jit(solution)/shard_map/ppermute | solution.py:136
  33.3 5.1 %legendre_sums.7 = (bf16[4,16,64,128]{3,2,1,0:T(8,128)(2,1)S(1)}, bf16[4,16,64,128]{3,2,1,0:T(8,128)(2,1)S(1)}, bf16[2,16,64,128]{3,2,1,0:T(8,128)(2,1)S(1)}, bf...) custom-call(s32[2]{0:T(128)S(1)} %get-tuple-element.99.place_ref, bf16[256,128,256]{2,1,0:T(8,128)(2,1)} %leg_ref.7, ...), custom_call_target="tpu_custom_call" | custom-call | tf_op jit(solution)/shard_map/legendre_sums/pallas_call | solution.py:55
  39.9 1.9 %collective-permute-start.7 = (bf16[4,16,64,128]{3,2,1,0:T(8,128)(2,1)S(1)}, bf16[4,16,64,128]{3,2,1,0:T(8,128)(2,1)S(1)}, u32[]{:S(2)}, u32[]{:S(2)}) collective-permute-start(bf16[4,16,64,128]{3,2,1,0:T(8,128)(2,1)S(1)} %get-tuple-element.67), channel_id=1, source_target_pairs={{0,96},{8,104},{16,112},{24,120},{32,64},{40,72},{48,80},{56,88},{... | collective-permute-start | bytes 3145736 | tf_op jit(solution)/shard_map/ppermute | solution.py:136
  41.8 4.2 %sine_multiply_fusion = (f32[2048,128]{1,0:T(8,128)S(1)}, f32[2048,128]{1,0:T(8,128)S(1)}) fusion(s32[2048]{0:T(1024)S(1)} %copy-done, f32[2048]{0:T(1024)S(1)} %get-tuple-element.98), kind=kLoop, calls=%fused_computation.6 | loop fusion | flops 4194304 | bytes 2113536 | tf_op jit(solution)/shard_map/mul | solution.py:195
  46.7 6.7 %build_tables.1 = (bf16[2048,1280]{1,0:T(8,128)(2,1)}, bf16[2048,1280]{1,0:T(8,128)(2,1)}) custom-call(bf16[2,16,64,128]{3,2,1,0:T(8,128)(2,1)S(1)} %get-tuple-element.52._.refs_3_, f32[2048,128]{1,0:T(8,128)S(1)} %get-tuple-element.94.cos_ref, f32[2048,128]{1,0:T(8,128)S(1)} %get-tuple-element.93.sin_ref, f32[2048,128]{1,0:T(8,128)S(1)} %broadcast_in_dim.20.cos_step, ...), custom_call_target="tpu_custom_call" | custom-call | tf_op jit(solution)/shard_map/build_tables/pallas_call | solution.py:187
  60.2 2.2 %collective-permute-done.7.refs_1_.refs_6_ = bf16[4,16,64,128]{3,2,1,0:T(8,128)(2,1)S(1)} collective-permute-done((bf16[4,16,64,128]{3,2,1,0:T(8,128)(2,1)S(1)}, bf16[4,16,64,128]{3,2,1,0:T(8,128)(2,1)S(1)}, u32[]{:S(2)}, u32[]{:S(2)}) %collective-permute-start.7) | collective-permute-done | bytes 1048608 | tf_op jit(solution)/shard_map/ppermute | solution.py:136
  62.7 2.0 %collective-permute-start.14 = (bf16[2,16,64,128]{3,2,1,0:T(8,128)(2,1)S(1)}, bf16[2,16,64,128]{3,2,1,0:T(8,128)(2,1)S(1)}, u32[]{:S(2)}, u32[]{:S(2)}) collective-permute-start(bf16[2,16,64,128]{3,2,1,0:T(8,128)(2,1)S(1)} %get-tuple-element.77), channel_id=1, source_target_pairs={{0,96},{8,104},{16,112},{24,120},{32,64},{40,72},{48,80},{56,88},{... | collective-permute-start | bytes 1572872 | tf_op jit(solution)/shard_map/ppermute | solution.py:136
  64.7 2.1 %collective-permute-done.10.refs_7_ = bf16[2,16,64,128]{3,2,1,0:T(8,128)(2,1)S(1)} collective-permute-done((bf16[2,16,64,128]{3,2,1,0:T(8,128)(2,1)S(1)}, bf16[2,16,64,128]{3,2,1,0:T(8,128)(2,1)S(1)}, u32[]{:S(2)}, u32[]{:S(2)}) %collective-permute-start.10) | collective-permute-done | bytes 524320 | tf_op jit(solution)/shard_map/ppermute | solution.py:136
  67.2 2.1 %collective-permute-start.12 = (bf16[2,16,64,128]{3,2,1,0:T(8,128)(2,1)}, bf16[2,16,64,128]{3,2,1,0:T(8,128)(2,1)S(1)}, u32[]{:S(2)}, u32[]{:S(2)}) collective-permute-start(bf16[2,16,64,128]{3,2,1,0:T(8,128)(2,1)} %get-tuple-element.75), channel_id=1, source_target_pairs={{0,96},{8,104},{16,112},{24,120},{32,64},{40,72},{48,80},{56,88},{... | collective-permute-start | bytes 1572872 | tf_op jit(solution)/shard_map/ppermute | solution.py:136
  69.3 8.7 %collective-permute-done.8.refs_2_ = bf16[2,16,64,128]{3,2,1,0:T(8,128)(2,1)S(1)} collective-permute-done((bf16[2,16,64,128]{3,2,1,0:T(8,128)(2,1)}, bf16[2,16,64,128]{3,2,1,0:T(8,128)(2,1)S(1)}, u32[]{:S(2)}, u32[]{:S(2)}) %collective-permute-start.8) | collective-permute-done | bytes 524320 | tf_op jit(solution)/shard_map/ppermute | solution.py:136
  81.9 2.6 %collective-permute-done.12.refs_2_ = bf16[2,16,64,128]{3,2,1,0:T(8,128)(2,1)S(1)} collective-permute-done((bf16[2,16,64,128]{3,2,1,0:T(8,128)(2,1)}, bf16[2,16,64,128]{3,2,1,0:T(8,128)(2,1)S(1)}, u32[]{:S(2)}, u32[]{:S(2)}) %collective-permute-start.12) | collective-permute-done | bytes 524320 | tf_op jit(solution)/shard_map/ppermute | solution.py:136
  84.5 7.6 %collective-permute-done.13.refs_3_ = bf16[2,16,64,128]{3,2,1,0:T(8,128)(2,1)S(1)} collective-permute-done((bf16[2,16,64,128]{3,2,1,0:T(8,128)(2,1)S(1)}, bf16[2,16,64,128]{3,2,1,0:T(8,128)(2,1)S(1)}, u32[]{:S(2)}, u32[]{:S(2)}) %collective-permute-start.13) | collective-permute-done | bytes 524320 | tf_op jit(solution)/shard_map/ppermute | solution.py:136
  94.2 9.1 %collective-permute-done.16.refs_0_ = bf16[16,128,128]{2,1,0:T(8,128)(2,1)S(1)} collective-permute-done((bf16[16,128,128]{2,1,0:T(8,128)(2,1)S(1)}, bf16[16,128,128]{2,1,0:T(8,128)(2,1)S(1)}, u32[]{:S(2)}, u32[]{:S(2)}) %collective-permute-start.16) | collective-permute-done | bytes 524320 | tf_op jit(solution)/shard_map/ppermute | solution.py:136
  104.9 2.8 %collective-permute-start.20 = (bf16[8,128,128]{2,1,0:T(8,128)(2,1)S(1)}, bf16[8,128,128]{2,1,0:T(8,128)(2,1)S(1)}, u32[]{:S(2)}, u32[]{:S(2)}) collective-permute-start(bf16[8,128,128]{2,1,0:T(8,128)(2,1)S(1)} %get-tuple-element.88), channel_id=1, source_target_pairs={{0,96},{8,104},{16,112},{24,120},{32,64},{40,72},{48,80},{56,88},{... | collective-permute-start | bytes 786440 | tf_op jit(solution)/shard_map/ppermute | solution.py:136
  107.6 4.7 %collective-permute-done.22.refs_7_ = bf16[8,128,128]{2,1,0:T(8,128)(2,1)S(1)} collective-permute-done((bf16[8,128,128]{2,1,0:T(8,128)(2,1)S(1)}, bf16[8,128,128]{2,1,0:T(8,128)(2,1)S(1)}, u32[]{:S(2)}, u32[]{:S(2)}) %collective-permute-start.22) | collective-permute-done | bytes 262176 | tf_op jit(solution)/shard_map/ppermute | solution.py:136
  114.2 17.2 %all-to-all-start = ((bf16[8,2,256,128]{3,2,1,0:T(8,128)(2,1)}), bf16[8,2,256,128]{3,2,1,0:T(8,128)(2,1)S(1)}, u32[]{:S(2)}, u32[]{:S(2)}) async-start(bf16[8,2,256,128]{3,2,1,0:T(8,128)(2,1)} %bitcast.2), calls=%async_computation | async-start | bytes 2097152 | tf_op jit(solution)/shard_map/all_to_all | solution.py:331
  131.4 15.0 %all-to-all-done.spec_ref = bf16[8,2,256,128]{3,2,1,0:T(8,128)(2,1)S(1)} async-done(((bf16[8,2,256,128]{3,2,1,0:T(8,128)(2,1)}), bf16[8,2,256,128]{3,2,1,0:T(8,128)(2,1)S(1)}, u32[]{:S(2)}, u32[]{:S(2)}) %all-to-all-start) | async-done | bytes 1048608 | tf_op jit(solution)/shard_map/all_to_all | solution.py:331
  146.5 8.5 %fourier_products.1 = bf16[2,32,4096]{2,1,0:T(8,128)(2,1)} custom-call(bf16[8,2,256,128]{3,2,1,0:T(8,128)(2,1)S(1)} %all-to-all-done.spec_ref, f32[8,2048]{1,0:T(8,128)S(1)} %broadcast_in_dim.42.even_ref, bf16[128,128]{1,0:T(8,128)(2,1)S(1)} %fusion.7.pick_ref, bf16[256,128]{1,0:T(8,128)(2,1)S(1)} %fusion.6.turn_ref, ...), custom_call_target="tpu_custom_call" | custom-call | tf_op jit(solution)/shard_map/fourier_products/pallas_call | solution.py:273
  (53 shorter events, 23.1 us)
Async XLA Ops:
  5.9 24.5 %collective-permute-start = (bf16[4,16,64,128]{3,2,1,0:T(8,128)(2,1)S(1)}, bf16[4,16,64,128]{3,2,1,0:T(8,128)(2,1)S(1)}, u32[]{:S(2)}, u32[]{:S(2)}) collective-permute-start(bf16[4,16,64,128]{3,2,1,0:T(8,128)(2,1)S(1)} %get-tuple-element.54), channel_id=1, source_target_pairs={{0,8},{8,0},{16,24},{24,16},{32,40},{40,32},{48,56},{56,48},{64,72... | collective-permute-start | bytes 3145736 | tf_op jit(solution)/shard_map/ppermute | solution.py:136
  8.0 30.4 %collective-permute-start.1 = (bf16[4,16,64,128]{3,2,1,0:T(8,128)(2,1)S(1)}, bf16[4,16,64,128]{3,2,1,0:T(8,128)(2,1)S(1)}, u32[]{:S(2)}, u32[]{:S(2)}) collective-permute-start(bf16[4,16,64,128]{3,2,1,0:T(8,128)(2,1)S(1)} %get-tuple-element.55), channel_id=1, source_target_pairs={{0,24},{8,16},{16,8},{24,0},{32,56},{40,48},{48,40},{56,32},{64,88... | collective-permute-start | bytes 3145736 | tf_op jit(solution)/shard_map/ppermute | solution.py:136
  15.5 24.3 %collective-permute-start.2 = (bf16[4,16,64,128]{3,2,1,0:T(8,128)(2,1)S(1)}, bf16[4,16,64,128]{3,2,1,0:T(8,128)(2,1)S(1)}, u32[]{:S(2)}, u32[]{:S(2)}) collective-permute-start(bf16[4,16,64,128]{3,2,1,0:T(8,128)(2,1)S(1)} %get-tuple-element.58), channel_id=1, source_target_pairs={{0,32},{8,40},{16,48},{24,56},{32,0},{40,8},{48,16},{56,24},{64,96... | collective-permute-start | bytes 3145736 | tf_op jit(solution)/shard_map/ppermute | solution.py:136
  16.8 37.5 %collective-permute-start.3 = (bf16[4,16,64,128]{3,2,1,0:T(8,128)(2,1)}, bf16[4,16,64,128]{3,2,1,0:T(8,128)(2,1)S(1)}, u32[]{:S(2)}, u32[]{:S(2)}) collective-permute-start(bf16[4,16,64,128]{3,2,1,0:T(8,128)(2,1)} %get-tuple-element.59), channel_id=1, source_target_pairs={{0,96},{8,104},{16,112},{24,120},{32,64},{40,72},{48,80},{56,88},{... | collective-permute-start | bytes 3145736 | tf_op jit(solution)/shard_map/ppermute | solution.py:136
  24.5 30.8 %collective-permute-start.4 = (bf16[4,16,64,128]{3,2,1,0:T(8,128)(2,1)}, bf16[4,16,64,128]{3,2,1,0:T(8,128)(2,1)S(1)}, u32[]{:S(2)}, u32[]{:S(2)}) collective-permute-start(bf16[4,16,64,128]{3,2,1,0:T(8,128)(2,1)} %get-tuple-element.62), channel_id=1, source_target_pairs={{0,8},{8,0},{16,24},{24,16},{32,40},{40,32},{48,56},{56,48},{64,72... | collective-permute-start | bytes 3145736 | tf_op jit(solution)/shard_map/ppermute | solution.py:136
  30.4 25.0 %collective-permute-start.5 = (bf16[4,16,64,128]{3,2,1,0:T(8,128)(2,1)}, bf16[4,16,64,128]{3,2,1,0:T(8,128)(2,1)S(1)}, u32[]{:S(2)}, u32[]{:S(2)}) collective-permute-start(bf16[4,16,64,128]{3,2,1,0:T(8,128)(2,1)} %get-tuple-element.63), channel_id=1, source_target_pairs={{0,24},{8,16},{16,8},{24,0},{32,56},{40,48},{48,40},{56,32},{64,88... | collective-permute-start | bytes 3145736 | tf_op jit(solution)/shard_map/ppermute | solution.py:136
  38.5 21.7 %collective-permute-start.6 = (bf16[4,16,64,128]{3,2,1,0:T(8,128)(2,1)S(1)}, bf16[4,16,64,128]{3,2,1,0:T(8,128)(2,1)S(1)}, u32[]{:S(2)}, u32[]{:S(2)}) collective-permute-start(bf16[4,16,64,128]{3,2,1,0:T(8,128)(2,1)S(1)} %get-tuple-element.66), channel_id=1, source_target_pairs={{0,32},{8,40},{16,48},{24,56},{32,0},{40,8},{48,16},{56,24},{64,96... | collective-permute-start | bytes 3145736 | tf_op jit(solution)/shard_map/ppermute | solution.py:136
  39.9 22.6 %collective-permute-start.7 = (bf16[4,16,64,128]{3,2,1,0:T(8,128)(2,1)S(1)}, bf16[4,16,64,128]{3,2,1,0:T(8,128)(2,1)S(1)}, u32[]{:S(2)}, u32[]{:S(2)}) collective-permute-start(bf16[4,16,64,128]{3,2,1,0:T(8,128)(2,1)S(1)} %get-tuple-element.67), channel_id=1, source_target_pairs={{0,96},{8,104},{16,112},{24,120},{32,64},{40,72},{48,80},{56,88},{... | collective-permute-start | bytes 3145736 | tf_op jit(solution)/shard_map/ppermute | solution.py:136
  55.6 11.2 %collective-permute-start.10 = (bf16[2,16,64,128]{3,2,1,0:T(8,128)(2,1)S(1)}, bf16[2,16,64,128]{3,2,1,0:T(8,128)(2,1)S(1)}, u32[]{:S(2)}, u32[]{:S(2)}) collective-permute-start(bf16[2,16,64,128]{3,2,1,0:T(8,128)(2,1)S(1)} %get-tuple-element.72), channel_id=1, source_target_pairs={{0,24},{8,16},{16,8},{24,0},{32,56},{40,48},{48,40},{56,32},{64,88... | collective-permute-start | bytes 1572872 | tf_op jit(solution)/shard_map/ppermute | solution.py:136
  57.0 10.2 %collective-permute-start.11 = (bf16[2,16,64,128]{3,2,1,0:T(8,128)(2,1)S(1)}, bf16[2,16,64,128]{3,2,1,0:T(8,128)(2,1)S(1)}, u32[]{:S(2)}, u32[]{:S(2)}) collective-permute-start(bf16[2,16,64,128]{3,2,1,0:T(8,128)(2,1)S(1)} %get-tuple-element.65._), channel_id=1, source_target_pairs={{0,8},{8,0},{16,24},{24,16},{32,40},{40,32},{48,56},{56,48},{64,72... | collective-permute-start | bytes 1572872 | tf_op jit(solution)/shard_map/ppermute | solution.py:136
  57.0 21.0 %collective-permute-start.8 = (bf16[2,16,64,128]{3,2,1,0:T(8,128)(2,1)}, bf16[2,16,64,128]{3,2,1,0:T(8,128)(2,1)S(1)}, u32[]{:S(2)}, u32[]{:S(2)}) collective-permute-start(bf16[2,16,64,128]{3,2,1,0:T(8,128)(2,1)} %get-tuple-element.70), channel_id=1, source_target_pairs={{0,24},{8,16},{16,8},{24,0},{32,56},{40,48},{48,40},{56,32},{64,88... | collective-permute-start | bytes 1572872 | tf_op jit(solution)/shard_map/ppermute | solution.py:136
  60.2 18.2 %collective-permute-start.9 = (bf16[2,16,64,128]{3,2,1,0:T(8,128)(2,1)S(1)}, bf16[2,16,64,128]{3,2,1,0:T(8,128)(2,1)S(1)}, u32[]{:S(2)}, u32[]{:S(2)}) collective-permute-start(bf16[2,16,64,128]{3,2,1,0:T(8,128)(2,1)S(1)} %get-tuple-element.57._), channel_id=1, source_target_pairs={{0,8},{8,0},{16,24},{24,16},{32,40},{40,32},{48,56},{56,48},{64,72... | collective-permute-start | bytes 1572872 | tf_op jit(solution)/shard_map/ppermute | solution.py:136
  62.7 17.6 %collective-permute-start.14 = (bf16[2,16,64,128]{3,2,1,0:T(8,128)(2,1)S(1)}, bf16[2,16,64,128]{3,2,1,0:T(8,128)(2,1)S(1)}, u32[]{:S(2)}, u32[]{:S(2)}) collective-permute-start(bf16[2,16,64,128]{3,2,1,0:T(8,128)(2,1)S(1)} %get-tuple-element.77), channel_id=1, source_target_pairs={{0,96},{8,104},{16,112},{24,120},{32,64},{40,72},{48,80},{56,88},{... | collective-permute-start | bytes 1572872 | tf_op jit(solution)/shard_map/ppermute | solution.py:136
  66.8 15.1 %collective-permute-start.15 = (bf16[2,16,64,128]{3,2,1,0:T(8,128)(2,1)S(1)}, bf16[2,16,64,128]{3,2,1,0:T(8,128)(2,1)S(1)}, u32[]{:S(2)}, u32[]{:S(2)}) collective-permute-start(bf16[2,16,64,128]{3,2,1,0:T(8,128)(2,1)S(1)} %get-tuple-element.69._), channel_id=1, source_target_pairs={{0,32},{8,40},{16,48},{24,56},{32,0},{40,8},{48,16},{56,24},{64,96... | collective-permute-start | bytes 1572872 | tf_op jit(solution)/shard_map/ppermute | solution.py:136
  67.2 17.3 %collective-permute-start.12 = (bf16[2,16,64,128]{3,2,1,0:T(8,128)(2,1)}, bf16[2,16,64,128]{3,2,1,0:T(8,128)(2,1)S(1)}, u32[]{:S(2)}, u32[]{:S(2)}) collective-permute-start(bf16[2,16,64,128]{3,2,1,0:T(8,128)(2,1)} %get-tuple-element.75), channel_id=1, source_target_pairs={{0,96},{8,104},{16,112},{24,120},{32,64},{40,72},{48,80},{56,88},{... | collective-permute-start | bytes 1572872 | tf_op jit(solution)/shard_map/ppermute | solution.py:136
  78.0 14.0 %collective-permute-start.13 = (bf16[2,16,64,128]{3,2,1,0:T(8,128)(2,1)S(1)}, bf16[2,16,64,128]{3,2,1,0:T(8,128)(2,1)S(1)}, u32[]{:S(2)}, u32[]{:S(2)}) collective-permute-start(bf16[2,16,64,128]{3,2,1,0:T(8,128)(2,1)S(1)} %get-tuple-element.61._), channel_id=1, source_target_pairs={{0,32},{8,40},{16,48},{24,56},{32,0},{40,8},{48,16},{56,24},{64,96... | collective-permute-start | bytes 1572872 | tf_op jit(solution)/shard_map/ppermute | solution.py:136
  79.2 24.1 %collective-permute-start.16 = (bf16[16,128,128]{2,1,0:T(8,128)(2,1)S(1)}, bf16[16,128,128]{2,1,0:T(8,128)(2,1)S(1)}, u32[]{:S(2)}, u32[]{:S(2)}) collective-permute-start(bf16[16,128,128]{2,1,0:T(8,128)(2,1)S(1)} %get-tuple-element.80), channel_id=1, source_target_pairs={{0,32},{8,40},{16,48},{24,56},{32,0},{40,8},{48,16},{56,24},{64,96... | collective-permute-start | bytes 1572872 | tf_op jit(solution)/shard_map/ppermute | solution.py:136
  80.3 22.9 %collective-permute-start.17 = (bf16[16,128,128]{2,1,0:T(8,128)(2,1)S(1)}, bf16[16,128,128]{2,1,0:T(8,128)(2,1)S(1)}, u32[]{:S(2)}, u32[]{:S(2)}) collective-permute-start(bf16[16,128,128]{2,1,0:T(8,128)(2,1)S(1)} %get-tuple-element.81), channel_id=1, source_target_pairs={{0,96},{8,104},{16,112},{24,120},{32,64},{40,72},{48,80},{56,88},{... | collective-permute-start | bytes 1572872 | tf_op jit(solution)/shard_map/ppermute | solution.py:136
  92.8 10.6 %collective-permute-start.18 = (bf16[16,128,128]{2,1,0:T(8,128)(2,1)S(1)}, bf16[16,128,128]{2,1,0:T(8,128)(2,1)S(1)}, u32[]{:S(2)}, u32[]{:S(2)}) collective-permute-start(bf16[16,128,128]{2,1,0:T(8,128)(2,1)S(1)} %get-tuple-element.84), channel_id=1, source_target_pairs={{0,8},{8,0},{16,24},{24,16},{32,40},{40,32},{48,56},{56,48},{64,72... | collective-permute-start | bytes 1572872 | tf_op jit(solution)/shard_map/ppermute | solution.py:136
  92.9 10.5 %collective-permute-start.19 = (bf16[16,128,128]{2,1,0:T(8,128)(2,1)S(1)}, bf16[16,128,128]{2,1,0:T(8,128)(2,1)S(1)}, u32[]{:S(2)}, u32[]{:S(2)}) collective-permute-start(bf16[16,128,128]{2,1,0:T(8,128)(2,1)S(1)} %get-tuple-element.85), channel_id=1, source_target_pairs={{0,24},{8,16},{16,8},{24,0},{32,56},{40,48},{48,40},{56,32},{64,88... | collective-permute-start | bytes 1572872 | tf_op jit(solution)/shard_map/ppermute | solution.py:136
  103.6 8.8 %collective-permute-start.22 = (bf16[8,128,128]{2,1,0:T(8,128)(2,1)S(1)}, bf16[8,128,128]{2,1,0:T(8,128)(2,1)S(1)}, u32[]{:S(2)}, u32[]{:S(2)}) collective-permute-start(bf16[8,128,128]{2,1,0:T(8,128)(2,1)S(1)} %get-tuple-element.90), channel_id=1, source_target_pairs={{0,24},{8,16},{16,8},{24,0},{32,56},{40,48},{48,40},{56,32},{64,88... | collective-permute-start | bytes 786440 | tf_op jit(solution)/shard_map/ppermute | solution.py:136
  104.9 7.5 %collective-permute-start.23 = (bf16[8,128,128]{2,1,0:T(8,128)(2,1)S(1)}, bf16[8,128,128]{2,1,0:T(8,128)(2,1)S(1)}, u32[]{:S(2)}, u32[]{:S(2)}) collective-permute-start(bf16[8,128,128]{2,1,0:T(8,128)(2,1)S(1)} %get-tuple-element.87._), channel_id=1, source_target_pairs={{0,8},{8,0},{16,24},{24,16},{32,40},{40,32},{48,56},{56,48},{64,72... | collective-permute-start | bytes 786440 | tf_op jit(solution)/shard_map/ppermute | solution.py:136
  104.9 7.5 %collective-permute-start.20 = (bf16[8,128,128]{2,1,0:T(8,128)(2,1)S(1)}, bf16[8,128,128]{2,1,0:T(8,128)(2,1)S(1)}, u32[]{:S(2)}, u32[]{:S(2)}) collective-permute-start(bf16[8,128,128]{2,1,0:T(8,128)(2,1)S(1)} %get-tuple-element.88), channel_id=1, source_target_pairs={{0,96},{8,104},{16,112},{24,120},{32,64},{40,72},{48,80},{56,88},{... | collective-permute-start | bytes 786440 | tf_op jit(solution)/shard_map/ppermute | solution.py:136
  114.2 32.3 %all-to-all-start = ((bf16[8,2,256,128]{3,2,1,0:T(8,128)(2,1)}), bf16[8,2,256,128]{3,2,1,0:T(8,128)(2,1)S(1)}, u32[]{:S(2)}, u32[]{:S(2)}) async-start(bf16[8,2,256,128]{3,2,1,0:T(8,128)(2,1)} %bitcast.2), calls=%async_computation | async-start | bytes 2097152 | tf_op jit(solution)/shard_map/all_to_all | solution.py:331
  (2 other events, 5.9 us)

commit v3 on v2

--- a/solution.py
+++ b/solution.py
@@ -15,7 +15,7 @@
 BF16 = jnp.bfloat16
 
 
-CHUNKS = 2
+CHUNKS = (48, 80)
 SIDE = 4
 
 
@@ -83,42 +83,29 @@
 
 
 def turn_kernel(*refs):
-    outs = refs[-5:]
-    first_out, second_out, third_out, one_out, own_out = outs
-    for c in range(CHUNKS):
+    outs = refs[-SIDE:]
+    start = 0
+    for c in range(len(CHUNKS)):
         got_first, got_second, last_first, last_second, own = refs[5 * c:5 * c + 5]
-        half = got_first.shape[0] // 2
-        rows, slots = own.shape[1] // 2, own.shape[2]
-        cols = pl.ds(c * slots, slots)
-
-        def sums(block, part):
+        half = SIDE // 2
+        slots = own.shape[2]
+        cols = pl.ds(start, slots)
+        start += slots
+        for block in range(SIDE):
             if block < half:
                 got, last, at = got_first, last_first, block
             else:
                 got, last, at = got_second, last_second, block - half
-            return add(own[block, part], got[at, part], last[at, part])
-
-        low, high = pl.ds(0, rows), pl.ds(rows, rows)
-        first_out[0:rows, cols] = sums(1, low)
-        first_out[rows:, cols] = sums(2, low)
-        second_out[0:rows, cols] = sums(3, high)
-        second_out[rows:, cols] = sums(2, high)
-        third_out[:, cols] = sums(3, low)
-        one_out[:, cols] = sums(1, high)
-        own_out[0:rows, cols] = sums(0, low)
-        own_out[rows:, cols] = sums(0, high)
+            outs[block][:, cols] = add(own[block], got[at], last[at])
 
 
 def join_kernel(*refs):
     out = refs[-1]
-    count = (len(refs) - 1) // 5
+    count = (len(refs) - 1) // SIDE
     slots = out.shape[1] // count
-    rows = out.shape[0] // 2
     for i in range(count):
-        got_first, got_second, last_first, last_second, own = refs[5 * i:5 * i + 5]
         cols = pl.ds(i * slots, slots)
-        out[0:rows, cols] = add(own[0:rows], got_first[0:rows], last_first[...])
-        out[rows:, cols] = add(own[rows:], got_second[0:rows], last_second[...])
+        out[:, cols] = add(*[ref[...] for ref in refs[SIDE * i:SIDE * i + SIDE]])
 
 
 def call(kernel, name, shapes, after, *arrays):
@@ -136,28 +123,37 @@
     return lax.ppermute(array, "deg", [(d, d ^ bits) for d in range(SIDE * SIDE)])
 
 
-def start_sums(parts, unit):
+def later(array, *before):
+    return lax.optimization_barrier((array, *before))[0]
+
+
+def start_sums(parts, unit, before=((), ())):
     first, second, third, one, own = parts
-    return exchange(first, unit), exchange(second, 3 * unit), third, one, own
-
-
-def pass_sums(state, unit, after):
+    return (
+        exchange(later(first, *before[0]), unit),
+        exchange(later(second, *before[1]), 3 * unit),
+        third, one, own,
+    )
+
+
+def pass_sums(state, unit, after, before=((), ())):
     got_first, got_second, third, one, own = state
     send_first, send_second = call(
         pass_kernel, "pass_sums", (third.shape, one.shape), after, got_first, got_second, third, one
     )
-    last_first = exchange(send_first, 3 * unit)
-    last_second = exchange(send_second, unit)
+    last_first = exchange(later(send_first, *before[1]), 3 * unit)
+    last_second = exchange(later(send_second, *before[0]), unit)
     return (got_first, got_second, last_first, last_second, own), send_second
 
 
 def turn_sums(states, unit, after):
-    rows, slots, channels = states[0][-1].shape[1:]
-    slots = slots * CHUNKS
-    whole, half = (rows, slots, channels), (rows // 2, slots, channels)
+    rows, _, channels = states[0][-1].shape[1:]
+    slots = sum(state[-1].shape[2] for state in states)
     arrays = [a for state in states for a in state]
-    parts = call(turn_kernel, "turn_sums", (whole, whole, half, half, whole), after, *arrays)
-    return start_sums(parts, unit), parts[3]
+    own, one, two, three = call(
+        turn_kernel, "turn_sums", ((rows, slots, channels),) * SIDE, after, *arrays
+    )
+    return (own, exchange(one, unit), exchange(three, 3 * unit), exchange(two, 2 * unit)), own
 
 
 def table_kernel(_, cos_ref, sin_ref, cos_step, sin_step, cos_out, sin_out):
@@ -299,33 +295,43 @@
     y, x = here // SIDE, here % SIDE
     total, channels = coefficients.shape[0], coefficients.shape[2]
     groups = order_table.shape[0] // total
-    slots = total // (2 * CHUNKS)
     coefficients = pltpu.with_memory_space_constraint(coefficients, pltpu.HBM)
     legendre = pltpu.with_memory_space_constraint(legendre, pltpu.HBM)
     units = ((1, SIDE), (SIDE, 1))
     state = {}
-    after = order_table
-    keys = [(k, way) for k in range(CHUNKS) for way in range(2)]
+    after = legendre
+    keys = [(k, way) for k in range(len(CHUNKS)) for way in range(2)]
+    parts = {}
     for k, way in keys:
         place = jnp.stack([x, y] if way == 0 else [y, x]).astype(jnp.int32)
-        parts = legendre_sums(
-            place, legendre, coefficients, after, (way * CHUNKS + k) * slots, slots, units[way]
+        start = way * sum(CHUNKS) + sum(CHUNKS[:k])
+        parts[k, way] = legendre_sums(
+            place, legendre, coefficients, after, start, CHUNKS[k], units[way]
         )
-        after = parts[3]
-        state[k, way] = start_sums(parts, units[way][0])
+        after = parts[k, way][3]
+    for k, way in keys:
+        before = ((), ())
+        if k:
+            got = state[k - 1, way]
+            before = ((got[0], after), (got[1], after))
+        state[k, way] = start_sums(parts[k, way], units[way][0], before)
     tables = build_tables(order_table, after)
     tables = [pltpu.with_memory_space_constraint(t, pltpu.HBM) for t in tables]
     after = tables[0]
     for k, way in keys:
-        state[k, way], after = pass_sums(state[k, way], units[way][0], after)
+        if k:
+            got = state[k - 1, way]
+            before = ((got[3],), (got[2],))
+        else:
+            got = state[k + 1, way]
+            before = ((got[0],), (got[1],))
+        state[k, way], after = pass_sums(state[k, way], units[way][0], after, before)
     ends = []
     for way in range(2):
-        end, after = turn_sums([state[k, way] for k in range(CHUNKS)], units[way][1], after)
+        end, after = turn_sums([state[k, way] for k in range(len(CHUNKS))], units[way][1], after)
         ends.append(end)
-    for way in range(2):
-        ends[way], after = pass_sums(ends[way], units[way][1], after)
     pair = ends[0] + ends[1]
-    rows = pair[-1].shape[0]
+    rows = pair[0].shape[0]
     (summed,) = call(join_kernel, "join_sums", ((rows, total, channels),), after, *pair)
     sent = summed.reshape(groups, rows // groups, total, channels)
     spectra = lax.all_to_all(sent, "ord", split_axis=0, concat_axis=0, tiled=True)

time: 155 us -> 146 us (0.942)
  starting transfers between devices: 46.6 us -> 41.9 us
  waiting for transfers between devices: 60.1 us -> 56.3 us
    all_to_all x1, starting transfers between devices: 17.2 us -> 12.5 us  [local(): lax.all_to_all(sent, 'ord', split_axis=0, concat_axis=0, tiled=True)]
    ppermute x24 -> x22, waiting for transfers between devices: 45 us -> 41.3 us  [exchange(): lax.ppermute(array, 'deg', [(d, d ^ bits) for d in range(SIDE * SIDE)])]
    pallas_call x9 -> x7, Pallas kernels: 5.51 us -> 5.27 us  [call(): pl.pallas_call(lambda _, *refs: kernel(*refs), out_shape=[jax.ShapeDtypeS...]
    ppermute x24 -> x22, starting transfers between devices: 29.4 us -> 29.5 us  [exchange(): lax.ppermute(array, 'deg', [(d, d ^ bits) for d in range(SIDE * SIDE)])]
  transfers between devices with their start and end apart: 25 -> 23, of which waited for: 11 -> 12; matrix products, arithmetic and copies ran while one was open for 3% -> 3% of each run, Pallas kernels for 18% -> 16%
where the time goes in v3:
time: 146 us
  waiting for transfers between devices  56.3 us (39%)
  Pallas kernels  42.5 us (29%)
  starting transfers between devices  41.9 us (29%)
  other arithmetic  4.38 us (3%)
    ppermute x22, waiting for transfers between devices, exchange(): lax.ppermute(array, 'deg', [(d, d ^ bits) for d in range(SIDE * SIDE)])  41.3 us
    ppermute x22, starting transfers between devices, exchange(): lax.ppermute(array, 'deg', [(d, d ^ bits) for d in range(SIDE * SIDE)])  29.5 us
    pallas_call x4, Pallas kernels, legendre_sums(): pl.pallas_call(functools.partial(legendre_kernel, strides=strides), out_s...  22 us
    all_to_all x1, waiting for transfers between devices, local(): lax.all_to_all(sent, 'ord', split_axis=0, concat_axis=0, tiled=True)  15 us
    all_to_all x1, starting transfers between devices, local(): lax.all_to_all(sent, 'ord', split_axis=0, concat_axis=0, tiled=True)  12.5 us
    pallas_call x1, Pallas kernels, fourier_products(): pl.pallas_call(fourier_kernel, out_shape=jax.ShapeDtypeStruct((lats, fiel...  8.51 us
    pallas_call x1, Pallas kernels, build_tables(): pl.pallas_call(table_kernel, out_shape=[pltpu.HBM((count, WIDE), BF16)] *...  6.68 us
    pallas_call x7, Pallas kernels, call(): pl.pallas_call(lambda _, *refs: kernel(*refs), out_shape=[jax.ShapeDtypeS...  5.27 us
  transfers between devices with their start and end apart: 23, of which 12 were waited for; matrix products, arithmetic and copies ran while one was open for 3% of the time, Pallas kernels for 16%

profile of v3, /device:TPU:1, one launch (start us, length us, event | category | flops | bytes accessed | tf_op | source)
XLA Modules:
  0.0 145.9 jit_solution(4609629161465717466)
XLA Ops:
  0.1 4.1 %legendre_sums.4 = (bf16[4,16,48,128]{3,2,1,0:T(8,128)(2,1)S(1)}, bf16[4,16,48,128]{3,2,1,0:T(8,128)(2,1)S(1)}, bf16[2,16,48,128]{3,2,1,0:T(8,128)(2,1)S(1)}, bf...) custom-call(s32[2]{0:T(128)S(1)} %get-tuple-element.112.place_ref, bf16[256,128,256]{2,1,0:T(8,128)(2,1)} %leg_ref.7, ...), custom_call_target="tpu_custom_call" | custom-call | tf_op jit(solution)/shard_map/legendre_sums/pallas_call | solution.py:55
  4.2 4.2 %legendre_sums.5 = (bf16[4,16,48,128]{3,2,1,0:T(8,128)(2,1)S(1)}, bf16[4,16,48,128]{3,2,1,0:T(8,128)(2,1)S(1)}, bf16[2,16,48,128]{3,2,1,0:T(8,128)(2,1)S(1)}, bf...) custom-call(s32[2]{0:T(128)S(1)} %get-tuple-element.111.place_ref, bf16[256,128,256]{2,1,0:T(8,128)(2,1)} %leg_ref.7, ...), custom_call_target="tpu_custom_call" | custom-call | tf_op jit(solution)/shard_map/legendre_sums/pallas_call | solution.py:55
  8.4 2.2 %collective-permute-start.2 = (bf16[4,16,48,128]{3,2,1,0:T(8,128)(2,1)S(1)}, bf16[4,16,48,128]{3,2,1,0:T(8,128)(2,1)S(1)}, u32[]{:S(2)}, u32[]{:S(2)}) collective-permute-start(bf16[4,16,48,128]{3,2,1,0:T(8,128)(2,1)S(1)} %get-tuple-element.64), channel_id=1, source_target_pairs={{0,32},{8,40},{16,48},{24,56},{32,0},{40,8},{48,16},{56,24},{64,96... | collective-permute-start | bytes 2359304 | tf_op jit(solution)/shard_map/ppermute | solution.py:123
  13.6 1.9 %collective-permute-start.3 = (bf16[4,16,48,128]{3,2,1,0:T(8,128)(2,1)S(1)}, bf16[4,16,48,128]{3,2,1,0:T(8,128)(2,1)S(1)}, u32[]{:S(2)}, u32[]{:S(2)}) collective-permute-start(bf16[4,16,48,128]{3,2,1,0:T(8,128)(2,1)S(1)} %get-tuple-element.65), channel_id=1, source_target_pairs={{0,96},{8,104},{16,112},{24,120},{32,64},{40,72},{48,80},{56,88},{... | collective-permute-start | bytes 2359304 | tf_op jit(solution)/shard_map/ppermute | solution.py:123
  15.5 6.9 %legendre_sums.6 = (bf16[4,16,80,128]{3,2,1,0:T(8,128)(2,1)}, bf16[4,16,80,128]{3,2,1,0:T(8,128)(2,1)S(1)}, bf16[2,16,80,128]{3,2,1,0:T(8,128)(2,1)S(1)}, bf16[2...) custom-call(s32[2]{0:T(128)S(1)} %get-tuple-element.112.place_ref, bf16[256,128,256]{2,1,0:T(8,128)(2,1)} %leg_ref.7, ...), custom_call_target="tpu_custom_call" | custom-call | tf_op jit(solution)/shard_map/legendre_sums/pallas_call | solution.py:55
  22.4 6.9 %legendre_sums.7 = (bf16[4,16,80,128]{3,2,1,0:T(8,128)(2,1)}, bf16[4,16,80,128]{3,2,1,0:T(8,128)(2,1)S(1)}, bf16[2,16,80,128]{3,2,1,0:T(8,128)(2,1)S(1)}, bf16[2...) custom-call(s32[2]{0:T(128)S(1)} %get-tuple-element.111.place_ref, bf16[256,128,256]{2,1,0:T(8,128)(2,1)} %leg_ref.7, ...), custom_call_target="tpu_custom_call" | custom-call | tf_op jit(solution)/shard_map/legendre_sums/pallas_call | solution.py:55
  32.6 1.9 %collective-permute-start.7 = (bf16[4,16,80,128]{3,2,1,0:T(8,128)(2,1)S(1)}, bf16[4,16,80,128]{3,2,1,0:T(8,128)(2,1)S(1)}, u32[]{:S(2)}, u32[]{:S(2)}) collective-permute-start(bf16[4,16,80,128]{3,2,1,0:T(8,128)(2,1)S(1)} %get-tuple-element.77), channel_id=1, source_target_pairs={{0,96},{8,104},{16,112},{24,120},{32,64},{40,72},{48,80},{56,88},{... | collective-permute-start | bytes 3932168 | tf_op jit(solution)/shard_map/ppermute | solution.py:123
  34.6 4.2 %sine_multiply_fusion = (f32[2048,128]{1,0:T(8,128)S(1)}, f32[2048,128]{1,0:T(8,128)S(1)}) fusion(s32[2048]{0:T(1024)S(1)} %copy-done, f32[2048]{0:T(1024)S(1)} %get-tuple-element.110), kind=kLoop, calls=%fused_computation.6 | loop fusion | flops 4194304 | bytes 2113536 | tf_op jit(solution)/shard_map/mul | solution.py:191
  39.5 6.7 %build_tables.1 = (bf16[2048,1280]{1,0:T(8,128)(2,1)}, bf16[2048,1280]{1,0:T(8,128)(2,1)}) custom-call(bf16[2,16,80,128]{3,2,1,0:T(8,128)(2,1)S(1)} %get-tuple-element.58._.refs_3_, f32[2048,128]{1,0:T(8,128)S(1)} %get-tuple-element.106.cos_ref, f32[2048,128]{1,0:T(8,128)S(1)} %get-tuple-element.105.sin_ref, f32[2048,128]{1,0:T(8,128)S(1)} %broadcast_in_dim.20.cos_step, ...), custom_call_target="tpu_custom_call" | custom-call | tf_op jit(solution)/shard_map/build_tables/pallas_call | solution.py:183
  47.8 10.1 %collective-permute-done.6.refs_0_.refs_5_ = bf16[4,16,80,128]{3,2,1,0:T(8,128)(2,1)S(1)} collective-permute-done((bf16[4,16,80,128]{3,2,1,0:T(8,128)(2,1)}, bf16[4,16,80,128]{3,2,1,0:T(8,128)(2,1)S(1)}, u32[]{:S(2)}, u32[]{:S(2)}) %collective-permute-start.6) | collective-permute-done | bytes 1310752 | tf_op jit(solution)/shard_map/ppermute | solution.py:123
  61.9 1.9 %collective-permute-start.12 = (bf16[2,16,48,128]{3,2,1,0:T(8,128)(2,1)}, bf16[2,16,48,128]{3,2,1,0:T(8,128)(2,1)S(1)}, u32[]{:S(2)}, u32[]{:S(2)}) collective-permute-start(bf16[2,16,48,128]{3,2,1,0:T(8,128)(2,1)} %get-tuple-element.90), channel_id=1, source_target_pairs={{0,96},{8,104},{16,112},{24,120},{32,64},{40,72},{48,80},{56,88},{... | collective-permute-start | bytes 1179656 | tf_op jit(solution)/shard_map/ppermute | solution.py:123
  67.2 1.9 %collective-permute-done.8.refs_2_ = bf16[2,16,48,128]{3,2,1,0:T(8,128)(2,1)S(1)} collective-permute-done((bf16[2,16,48,128]{3,2,1,0:T(8,128)(2,1)}, bf16[2,16,48,128]{3,2,1,0:T(8,128)(2,1)S(1)}, u32[]{:S(2)}, u32[]{:S(2)}) %collective-permute-start.8) | collective-permute-done | bytes 393248 | tf_op jit(solution)/shard_map/ppermute | solution.py:123
  70.9 1.9 %collective-permute-start.14 = (bf16[2,16,80,128]{3,2,1,0:T(8,128)(2,1)S(1)}, bf16[2,16,80,128]{3,2,1,0:T(8,128)(2,1)S(1)}, u32[]{:S(2)}, u32[]{:S(2)}) collective-permute-start(bf16[2,16,80,128]{3,2,1,0:T(8,128)(2,1)S(1)} %get-tuple-element.94), channel_id=1, source_target_pairs={{0,96},{8,104},{16,112},{24,120},{32,64},{40,72},{48,80},{56,88},{... | collective-permute-start | bytes 1966088 | tf_op jit(solution)/shard_map/ppermute | solution.py:123
  72.8 6.4 %collective-permute-done.11.refs_8_ = bf16[2,16,80,128]{3,2,1,0:T(8,128)(2,1)S(1)} collective-permute-done((bf16[2,16,80,128]{3,2,1,0:T(8,128)(2,1)S(1)}, bf16[2,16,80,128]{3,2,1,0:T(8,128)(2,1)S(1)}, u32[]{:S(2)}, u32[]{:S(2)}) %collective-permute-start.11) | collective-permute-done | bytes 655392 | tf_op jit(solution)/shard_map/ppermute | solution.py:123
  79.2 3.3 %collective-permute-done.10.refs_7_ = bf16[2,16,80,128]{3,2,1,0:T(8,128)(2,1)S(1)} collective-permute-done((bf16[2,16,80,128]{3,2,1,0:T(8,128)(2,1)S(1)}, bf16[2,16,80,128]{3,2,1,0:T(8,128)(2,1)S(1)}, u32[]{:S(2)}, u32[]{:S(2)}) %collective-permute-start.10) | collective-permute-done | bytes 655392 | tf_op jit(solution)/shard_map/ppermute | solution.py:123
  86.0 2.1 %collective-permute-start.21 = (bf16[16,128,128]{2,1,0:T(8,128)(2,1)S(1)}, bf16[16,128,128]{2,1,0:T(8,128)(2,1)S(1)}, u32[]{:S(2)}, u32[]{:S(2)}) collective-permute-start(bf16[16,128,128]{2,1,0:T(8,128)(2,1)S(1)} %get-tuple-element.103), channel_id=1, source_target_pairs={{0,16},{8,24},{16,0},{24,8},{32,48},{40,56},{48,32},{56,40},{64,80... | collective-permute-start | bytes 1572872 | tf_op jit(solution)/shard_map/ppermute | solution.py:123
  88.1 2.1 %collective-permute-start.17 = (bf16[16,128,128]{2,1,0:T(8,128)(2,1)S(1)}, bf16[16,128,128]{2,1,0:T(8,128)(2,1)S(1)}, u32[]{:S(2)}, u32[]{:S(2)}) collective-permute-start(bf16[16,128,128]{2,1,0:T(8,128)(2,1)S(1)} %get-tuple-element.99), channel_id=1, source_target_pairs={{0,96},{8,104},{16,112},{24,120},{32,64},{40,72},{48,80},{56,88},{... | collective-permute-start | bytes 1572872 | tf_op jit(solution)/shard_map/ppermute | solution.py:123
  90.3 2.6 %collective-permute-done.19.refs_5_ = bf16[16,128,128]{2,1,0:T(8,128)(2,1)S(1)} collective-permute-done((bf16[16,128,128]{2,1,0:T(8,128)(2,1)S(1)}, bf16[16,128,128]{2,1,0:T(8,128)(2,1)S(1)}, u32[]{:S(2)}, u32[]{:S(2)}) %collective-permute-start.19) | collective-permute-done | bytes 524320 | tf_op jit(solution)/shard_map/ppermute | solution.py:123
  92.9 2.3 %collective-permute-start.18 = (bf16[16,128,128]{2,1,0:T(8,128)(2,1)S(1)}, bf16[16,128,128]{2,1,0:T(8,128)(2,1)S(1)}, u32[]{:S(2)}, u32[]{:S(2)}) collective-permute-start(bf16[16,128,128]{2,1,0:T(8,128)(2,1)S(1)} %get-tuple-element.100), channel_id=1, source_target_pairs={{0,64},{8,72},{16,80},{24,88},{32,96},{40,104},{48,112},{56,120},{... | collective-permute-start | bytes 1572872 | tf_op jit(solution)/shard_map/ppermute | solution.py:123
  95.2 10.1 %collective-permute-done.21.refs_7_ = bf16[16,128,128]{2,1,0:T(8,128)(2,1)S(1)} collective-permute-done((bf16[16,128,128]{2,1,0:T(8,128)(2,1)S(1)}, bf16[16,128,128]{2,1,0:T(8,128)(2,1)S(1)}, u32[]{:S(2)}, u32[]{:S(2)}) %collective-permute-start.21) | collective-permute-done | bytes 524320 | tf_op jit(solution)/shard_map/ppermute | solution.py:123
  105.3 3.0 %collective-permute-done.18.refs_3_ = bf16[16,128,128]{2,1,0:T(8,128)(2,1)S(1)} collective-permute-done((bf16[16,128,128]{2,1,0:T(8,128)(2,1)S(1)}, bf16[16,128,128]{2,1,0:T(8,128)(2,1)S(1)}, u32[]{:S(2)}, u32[]{:S(2)}) %collective-permute-start.18) | collective-permute-done | bytes 524320 | tf_op jit(solution)/shard_map/ppermute | solution.py:123
  109.8 12.5 %all-to-all-start = ((bf16[8,2,256,128]{3,2,1,0:T(8,128)(2,1)}), bf16[8,2,256,128]{3,2,1,0:T(8,128)(2,1)S(1)}, u32[]{:S(2)}, u32[]{:S(2)}) async-start(bf16[8,2,256,128]{3,2,1,0:T(8,128)(2,1)} %bitcast.2), calls=%async_computation | async-start | bytes 2097152 | tf_op jit(solution)/shard_map/all_to_all | solution.py:337
  122.4 15.0 %all-to-all-done.spec_ref = bf16[8,2,256,128]{3,2,1,0:T(8,128)(2,1)S(1)} async-done(((bf16[8,2,256,128]{3,2,1,0:T(8,128)(2,1)}), bf16[8,2,256,128]{3,2,1,0:T(8,128)(2,1)S(1)}, u32[]{:S(2)}, u32[]{:S(2)}) %all-to-all-start) | async-done | bytes 1048608 | tf_op jit(solution)/shard_map/all_to_all | solution.py:337
  137.4 8.5 %fourier_products.1 = bf16[2,32,4096]{2,1,0:T(8,128)(2,1)} custom-call(bf16[8,2,256,128]{3,2,1,0:T(8,128)(2,1)S(1)} %all-to-all-done.spec_ref, f32[8,2048]{1,0:T(8,128)S(1)} %broadcast_in_dim.42.even_ref, bf16[128,128]{1,0:T(8,128)(2,1)S(1)} %fusion.7.pick_ref, bf16[256,128]{1,0:T(8,128)(2,1)S(1)} %fusion.6.turn_ref, ...), custom_call_target="tpu_custom_call" | custom-call | tf_op jit(solution)/shard_map/fourier_products/pallas_call | solution.py:269
  (47 shorter events, 23.0 us)
Async XLA Ops:
  8.4 20.9 %collective-permute-start.2 = (bf16[4,16,48,128]{3,2,1,0:T(8,128)(2,1)S(1)}, bf16[4,16,48,128]{3,2,1,0:T(8,128)(2,1)S(1)}, u32[]{:S(2)}, u32[]{:S(2)}) collective-permute-start(bf16[4,16,48,128]{3,2,1,0:T(8,128)(2,1)S(1)} %get-tuple-element.64), channel_id=1, source_target_pairs={{0,32},{8,40},{16,48},{24,56},{32,0},{40,8},{48,16},{56,24},{64,96... | collective-permute-start | bytes 2359304 | tf_op jit(solution)/shard_map/ppermute | solution.py:123
  10.6 19.1 %collective-permute-start = (bf16[4,16,48,128]{3,2,1,0:T(8,128)(2,1)S(1)}, bf16[4,16,48,128]{3,2,1,0:T(8,128)(2,1)S(1)}, u32[]{:S(2)}, u32[]{:S(2)}) collective-permute-start(bf16[4,16,48,128]{3,2,1,0:T(8,128)(2,1)S(1)} %get-tuple-element.60), channel_id=1, source_target_pairs={{0,8},{8,0},{16,24},{24,16},{32,40},{40,32},{48,56},{56,48},{64,72... | collective-permute-start | bytes 2359304 | tf_op jit(solution)/shard_map/ppermute | solution.py:123
  11.8 19.0 %collective-permute-start.1 = (bf16[4,16,48,128]{3,2,1,0:T(8,128)(2,1)S(1)}, bf16[4,16,48,128]{3,2,1,0:T(8,128)(2,1)S(1)}, u32[]{:S(2)}, u32[]{:S(2)}) collective-permute-start(bf16[4,16,48,128]{3,2,1,0:T(8,128)(2,1)S(1)} %get-tuple-element.61), channel_id=1, source_target_pairs={{0,24},{8,16},{16,8},{24,0},{32,56},{40,48},{48,40},{56,32},{64,88... | collective-permute-start | bytes 2359304 | tf_op jit(solution)/shard_map/ppermute | solution.py:123
  13.6 19.0 %collective-permute-start.3 = (bf16[4,16,48,128]{3,2,1,0:T(8,128)(2,1)S(1)}, bf16[4,16,48,128]{3,2,1,0:T(8,128)(2,1)S(1)}, u32[]{:S(2)}, u32[]{:S(2)}) collective-permute-start(bf16[4,16,48,128]{3,2,1,0:T(8,128)(2,1)S(1)} %get-tuple-element.65), channel_id=1, source_target_pairs={{0,96},{8,104},{16,112},{24,120},{32,64},{40,72},{48,80},{56,88},{... | collective-permute-start | bytes 2359304 | tf_op jit(solution)/shard_map/ppermute | solution.py:123
  22.4 12.2 %copy-start = (s32[2048]{0:T(1024)S(1)}, s32[2048]{0:T(1024)}, u32[]{:S(2)}) copy-start(s32[2048]{0:T(1024)} %param.5) | copy-start | bytes 24580
  29.3 28.7 %collective-permute-start.6 = (bf16[4,16,80,128]{3,2,1,0:T(8,128)(2,1)}, bf16[4,16,80,128]{3,2,1,0:T(8,128)(2,1)S(1)}, u32[]{:S(2)}, u32[]{:S(2)}) collective-permute-start(bf16[4,16,80,128]{3,2,1,0:T(8,128)(2,1)} %get-tuple-element.75), channel_id=1, source_target_pairs={{0,32},{8,40},{16,48},{24,56},{32,0},{40,8},{48,16},{56,24},{64,96... | collective-permute-start | bytes 3932168 | tf_op jit(solution)/shard_map/ppermute | solution.py:123
  29.7 28.7 %collective-permute-start.4 = (bf16[4,16,80,128]{3,2,1,0:T(8,128)(2,1)}, bf16[4,16,80,128]{3,2,1,0:T(8,128)(2,1)S(1)}, u32[]{:S(2)}, u32[]{:S(2)}) collective-permute-start(bf16[4,16,80,128]{3,2,1,0:T(8,128)(2,1)} %get-tuple-element.69), channel_id=1, source_target_pairs={{0,8},{8,0},{16,24},{24,16},{32,40},{40,32},{48,56},{56,48},{64,72... | collective-permute-start | bytes 3932168 | tf_op jit(solution)/shard_map/ppermute | solution.py:123
  30.8 29.3 %collective-permute-start.5 = (bf16[4,16,80,128]{3,2,1,0:T(8,128)(2,1)S(1)}, bf16[4,16,80,128]{3,2,1,0:T(8,128)(2,1)S(1)}, u32[]{:S(2)}, u32[]{:S(2)}) collective-permute-start(bf16[4,16,80,128]{3,2,1,0:T(8,128)(2,1)S(1)} %get-tuple-element.71), channel_id=1, source_target_pairs={{0,24},{8,16},{16,8},{24,0},{32,56},{40,48},{48,40},{56,32},{64,88... | collective-permute-start | bytes 3932168 | tf_op jit(solution)/shard_map/ppermute | solution.py:123
  32.6 29.3 %collective-permute-start.7 = (bf16[4,16,80,128]{3,2,1,0:T(8,128)(2,1)S(1)}, bf16[4,16,80,128]{3,2,1,0:T(8,128)(2,1)S(1)}, u32[]{:S(2)}, u32[]{:S(2)}) collective-permute-start(bf16[4,16,80,128]{3,2,1,0:T(8,128)(2,1)S(1)} %get-tuple-element.77), channel_id=1, source_target_pairs={{0,96},{8,104},{16,112},{24,120},{32,64},{40,72},{48,80},{56,88},{... | collective-permute-start | bytes 3932168 | tf_op jit(solution)/shard_map/ppermute | solution.py:123
  58.0 7.9 %collective-permute-start.13 = (bf16[2,16,48,128]{3,2,1,0:T(8,128)(2,1)S(1)}, bf16[2,16,48,128]{3,2,1,0:T(8,128)(2,1)S(1)}, u32[]{:S(2)}, u32[]{:S(2)}) collective-permute-start(bf16[2,16,48,128]{3,2,1,0:T(8,128)(2,1)S(1)} %get-tuple-element.91._), channel_id=1, source_target_pairs={{0,32},{8,40},{16,48},{24,56},{32,0},{40,8},{48,16},{56,24},{64,96... | collective-permute-start | bytes 1179656 | tf_op jit(solution)/shard_map/ppermute | solution.py:123
  58.4 7.9 %collective-permute-start.9 = (bf16[2,16,48,128]{3,2,1,0:T(8,128)(2,1)S(1)}, bf16[2,16,48,128]{3,2,1,0:T(8,128)(2,1)S(1)}, u32[]{:S(2)}, u32[]{:S(2)}) collective-permute-start(bf16[2,16,48,128]{3,2,1,0:T(8,128)(2,1)S(1)} %get-tuple-element.82._), channel_id=1, source_target_pairs={{0,8},{8,0},{16,24},{24,16},{32,40},{40,32},{48,56},{56,48},{64,72... | collective-permute-start | bytes 1179656 | tf_op jit(solution)/shard_map/ppermute | solution.py:123
  60.1 9.0 %collective-permute-start.8 = (bf16[2,16,48,128]{3,2,1,0:T(8,128)(2,1)}, bf16[2,16,48,128]{3,2,1,0:T(8,128)(2,1)S(1)}, u32[]{:S(2)}, u32[]{:S(2)}) collective-permute-start(bf16[2,16,48,128]{3,2,1,0:T(8,128)(2,1)} %get-tuple-element.81), channel_id=1, source_target_pairs={{0,24},{8,16},{16,8},{24,0},{32,56},{40,48},{48,40},{56,32},{64,88... | collective-permute-start | bytes 1179656 | tf_op jit(solution)/shard_map/ppermute | solution.py:123
  61.9 9.0 %collective-permute-start.12 = (bf16[2,16,48,128]{3,2,1,0:T(8,128)(2,1)}, bf16[2,16,48,128]{3,2,1,0:T(8,128)(2,1)S(1)}, u32[]{:S(2)}, u32[]{:S(2)}) collective-permute-start(bf16[2,16,48,128]{3,2,1,0:T(8,128)(2,1)} %get-tuple-element.90), channel_id=1, source_target_pairs={{0,96},{8,104},{16,112},{24,120},{32,64},{40,72},{48,80},{56,88},{... | collective-permute-start | bytes 1179656 | tf_op jit(solution)/shard_map/ppermute | solution.py:123
  65.8 17.4 %collective-permute-start.15 = (bf16[2,16,80,128]{3,2,1,0:T(8,128)(2,1)S(1)}, bf16[2,16,80,128]{3,2,1,0:T(8,128)(2,1)S(1)}, u32[]{:S(2)}, u32[]{:S(2)}) collective-permute-start(bf16[2,16,80,128]{3,2,1,0:T(8,128)(2,1)S(1)} %get-tuple-element.95._), channel_id=1, source_target_pairs={{0,32},{8,40},{16,48},{24,56},{32,0},{40,8},{48,16},{56,24},{64,96... | collective-permute-start | bytes 1966088 | tf_op jit(solution)/shard_map/ppermute | solution.py:123
  66.3 12.9 %collective-permute-start.11 = (bf16[2,16,80,128]{3,2,1,0:T(8,128)(2,1)S(1)}, bf16[2,16,80,128]{3,2,1,0:T(8,128)(2,1)S(1)}, u32[]{:S(2)}, u32[]{:S(2)}) collective-permute-start(bf16[2,16,80,128]{3,2,1,0:T(8,128)(2,1)S(1)} %get-tuple-element.86._), channel_id=1, source_target_pairs={{0,8},{8,0},{16,24},{24,16},{32,40},{40,32},{48,56},{56,48},{64,72... | collective-permute-start | bytes 1966088 | tf_op jit(solution)/shard_map/ppermute | solution.py:123
  69.1 13.4 %collective-permute-start.10 = (bf16[2,16,80,128]{3,2,1,0:T(8,128)(2,1)S(1)}, bf16[2,16,80,128]{3,2,1,0:T(8,128)(2,1)S(1)}, u32[]{:S(2)}, u32[]{:S(2)}) collective-permute-start(bf16[2,16,80,128]{3,2,1,0:T(8,128)(2,1)S(1)} %get-tuple-element.85), channel_id=1, source_target_pairs={{0,24},{8,16},{16,8},{24,0},{32,56},{40,48},{48,40},{56,32},{64,88... | collective-permute-start | bytes 1966088 | tf_op jit(solution)/shard_map/ppermute | solution.py:123
  70.9 13.2 %collective-permute-start.14 = (bf16[2,16,80,128]{3,2,1,0:T(8,128)(2,1)S(1)}, bf16[2,16,80,128]{3,2,1,0:T(8,128)(2,1)S(1)}, u32[]{:S(2)}, u32[]{:S(2)}) collective-permute-start(bf16[2,16,80,128]{3,2,1,0:T(8,128)(2,1)S(1)} %get-tuple-element.94), channel_id=1, source_target_pairs={{0,96},{8,104},{16,112},{24,120},{32,64},{40,72},{48,80},{56,88},{... | collective-permute-start | bytes 1966088 | tf_op jit(solution)/shard_map/ppermute | solution.py:123
  84.8 8.1 %collective-permute-start.19 = (bf16[16,128,128]{2,1,0:T(8,128)(2,1)S(1)}, bf16[16,128,128]{2,1,0:T(8,128)(2,1)S(1)}, u32[]{:S(2)}, u32[]{:S(2)}) collective-permute-start(bf16[16,128,128]{2,1,0:T(8,128)(2,1)S(1)} %get-tuple-element.101), channel_id=1, source_target_pairs={{0,8},{8,0},{16,24},{24,16},{32,40},{40,32},{48,56},{56,48},{64,72... | collective-permute-start | bytes 1572872 | tf_op jit(solution)/shard_map/ppermute | solution.py:123
  84.9 10.3 %collective-permute-start.20 = (bf16[16,128,128]{2,1,0:T(8,128)(2,1)S(1)}, bf16[16,128,128]{2,1,0:T(8,128)(2,1)S(1)}, u32[]{:S(2)}, u32[]{:S(2)}) collective-permute-start(bf16[16,128,128]{2,1,0:T(8,128)(2,1)S(1)} %get-tuple-element.102), channel_id=1, source_target_pairs={{0,24},{8,16},{16,8},{24,0},{32,56},{40,48},{48,40},{56,32},{64,88... | collective-permute-start | bytes 1572872 | tf_op jit(solution)/shard_map/ppermute | solution.py:123
  86.0 19.3 %collective-permute-start.21 = (bf16[16,128,128]{2,1,0:T(8,128)(2,1)S(1)}, bf16[16,128,128]{2,1,0:T(8,128)(2,1)S(1)}, u32[]{:S(2)}, u32[]{:S(2)}) collective-permute-start(bf16[16,128,128]{2,1,0:T(8,128)(2,1)S(1)} %get-tuple-element.103), channel_id=1, source_target_pairs={{0,16},{8,24},{16,0},{24,8},{32,48},{40,56},{48,32},{56,40},{64,80... | collective-permute-start | bytes 1572872 | tf_op jit(solution)/shard_map/ppermute | solution.py:123
  88.1 17.2 %collective-permute-start.16 = (bf16[16,128,128]{2,1,0:T(8,128)(2,1)S(1)}, bf16[16,128,128]{2,1,0:T(8,128)(2,1)S(1)}, u32[]{:S(2)}, u32[]{:S(2)}) collective-permute-start(bf16[16,128,128]{2,1,0:T(8,128)(2,1)S(1)} %get-tuple-element.98), channel_id=1, source_target_pairs={{0,32},{8,40},{16,48},{24,56},{32,0},{40,8},{48,16},{56,24},{64,96... | collective-permute-start | bytes 1572872 | tf_op jit(solution)/shard_map/ppermute | solution.py:123
  88.1 17.2 %collective-permute-start.17 = (bf16[16,128,128]{2,1,0:T(8,128)(2,1)S(1)}, bf16[16,128,128]{2,1,0:T(8,128)(2,1)S(1)}, u32[]{:S(2)}, u32[]{:S(2)}) collective-permute-start(bf16[16,128,128]{2,1,0:T(8,128)(2,1)S(1)} %get-tuple-element.99), channel_id=1, source_target_pairs={{0,96},{8,104},{16,112},{24,120},{32,64},{40,72},{48,80},{56,88},{... | collective-permute-start | bytes 1572872 | tf_op jit(solution)/shard_map/ppermute | solution.py:123
  92.9 15.4 %collective-permute-start.18 = (bf16[16,128,128]{2,1,0:T(8,128)(2,1)S(1)}, bf16[16,128,128]{2,1,0:T(8,128)(2,1)S(1)}, u32[]{:S(2)}, u32[]{:S(2)}) collective-permute-start(bf16[16,128,128]{2,1,0:T(8,128)(2,1)S(1)} %get-tuple-element.100), channel_id=1, source_target_pairs={{0,64},{8,72},{16,80},{24,88},{32,96},{40,104},{48,112},{56,120},{... | collective-permute-start | bytes 1572872 | tf_op jit(solution)/shard_map/ppermute | solution.py:123
  109.8 27.6 %all-to-all-start = ((bf16[8,2,256,128]{3,2,1,0:T(8,128)(2,1)}), bf16[8,2,256,128]{3,2,1,0:T(8,128)(2,1)S(1)}, u32[]{:S(2)}, u32[]{:S(2)}) async-start(bf16[8,2,256,128]{3,2,1,0:T(8,128)(2,1)} %bitcast.2), calls=%async_computation | async-start | bytes 2097152 | tf_op jit(solution)/shard_map/all_to_all | solution.py:337

commit v4 on v3

--- a/solution.py
+++ b/solution.py
@@ -10,7 +10,8 @@
 
 NLON = 4096
 QUARTER = NLON // 4
-WIDE = QUARTER + 256
+BLOCK = 256
+WIDE = QUARTER + BLOCK
 F32 = jnp.float32
 BF16 = jnp.bfloat16
 
@@ -99,13 +100,44 @@
             outs[block][:, cols] = add(own[block], got[at], last[at])
 
 
+def halve_kernel(*refs):
+    outs = refs[-5:]
+    first_out, second_out, third_out, one_out, own_out = outs
+    start = 0
+    for c in range(len(CHUNKS)):
+        got_first, got_second, last_first, last_second, own = refs[5 * c:5 * c + 5]
+        half = got_first.shape[0] // 2
+        rows, slots = own.shape[1] // 2, own.shape[2]
+        cols = pl.ds(start, slots)
+        start += slots
+
+        def sums(block, part):
+            if block < half:
+                got, last, at = got_first, last_first, block
+            else:
+                got, last, at = got_second, last_second, block - half
+            return add(own[block, part], got[at, part], last[at, part])
+
+        low, high = pl.ds(0, rows), pl.ds(rows, rows)
+        first_out[0:rows, cols] = sums(1, low)
+        first_out[rows:, cols] = sums(2, low)
+        second_out[0:rows, cols] = sums(3, high)
+        second_out[rows:, cols] = sums(2, high)
+        third_out[:, cols] = sums(3, low)
+        one_out[:, cols] = sums(1, high)
+        own_out[0:rows, cols] = sums(0, low)
+        own_out[rows:, cols] = sums(0, high)
+
+
 def join_kernel(*refs):
     out = refs[-1]
-    count = (len(refs) - 1) // SIDE
-    slots = out.shape[1] // count
-    for i in range(count):
-        cols = pl.ds(i * slots, slots)
-        out[:, cols] = add(*[ref[...] for ref in refs[SIDE * i:SIDE * i + SIDE]])
+    slots = out.shape[1] // 2
+    rows = out.shape[0] // 2
+    out[:, 0:slots] = add(*[ref[...] for ref in refs[:SIDE]])
+    got_first, got_second, last_first, last_second, own = refs[SIDE:-1]
+    cols = pl.ds(slots, slots)
+    out[0:rows, cols] = add(own[0:rows], got_first[0:rows], last_first[...])
+    out[rows:, cols] = add(own[rows:], got_second[0:rows], last_second[...])
 
 
 def call(kernel, name, shapes, after, *arrays):
@@ -156,14 +188,24 @@
     return (own, exchange(one, unit), exchange(three, 3 * unit), exchange(two, 2 * unit)), own
 
 
+def halve_sums(states, unit, after):
+    rows, _, channels = states[0][-1].shape[1:]
+    slots = sum(state[-1].shape[2] for state in states)
+    whole, half = (rows, slots, channels), (rows // 2, slots, channels)
+    arrays = [a for state in states for a in state]
+    parts = call(halve_kernel, "halve_sums", (whole, whole, half, half, whole), after, *arrays)
+    return pass_sums(start_sums(parts, unit), unit, parts[3])
+
+
 def table_kernel(_, cos_ref, sin_ref, cos_step, sin_step, cos_out, sin_out):
     c = cos_ref[...]
     s = sin_ref[...]
     dc = cos_step[...]
     ds = sin_step[...]
     for q in range(WIDE // 128):
-        cos_out[:, pl.ds(128 * q, 128)] = c.astype(BF16)
-        sin_out[:, pl.ds(128 * q, 128)] = (-s).astype(BF16)
+        cols = pl.ds(128 * q % BLOCK, 128)
+        cos_out[128 * q // BLOCK, :, cols] = c.astype(BF16)
+        sin_out[128 * q // BLOCK, :, cols] = (-s).astype(BF16)
         if q + 1 < WIDE // 128:
             c, s = c * dc - s * ds, s * dc + c * ds
 
@@ -179,10 +221,10 @@
     sin_big = jnp.broadcast_to(jnp.sin(big)[:, None], (count, 128))
     rows = 256
     narrow = pl.BlockSpec((rows, 128), lambda i: (i, 0))
-    wide = pl.BlockSpec((rows, WIDE), lambda i: (i, 0))
+    wide = pl.BlockSpec((WIDE // BLOCK, rows, BLOCK), lambda i: (0, i, 0))
     return pl.pallas_call(
         table_kernel,
-        out_shape=[pltpu.HBM((count, WIDE), BF16)] * 2,
+        out_shape=[pltpu.HBM((WIDE // BLOCK, count, BLOCK), BF16)] * 2,
         grid=(count // rows,),
         in_specs=[pl.BlockSpec(memory_space=pl.ANY)] + [narrow] * 4,
         out_specs=[wide] * 2,
@@ -191,65 +233,69 @@
     )(after, weight * jnp.cos(small), weight * jnp.sin(small), cos_big, sin_big)
 
 
-def fourier_kernel(spec_ref, even_ref, pick_ref, turn_ref, cos_ref, sin_ref, out_ref,
-                   left_cos, left_sin, plus, minus):
+def fourier_kernel(spec_ref, even_ref, pick_ref, turn_ref, cos_hbm, sin_hbm, out_ref,
+                   left_cos, left_sin, plus, minus, cos_ref, sin_ref, cos_sems, sin_sems):
+    copies = []
+    for b in range(WIDE // BLOCK):
+        copies.append((
+            pltpu.make_async_copy(cos_hbm.at[b], cos_ref.at[b], cos_sems.at[b]),
+            pltpu.make_async_copy(sin_hbm.at[b], sin_ref.at[b], sin_sems.at[b]),
+        ))
     blocks, lats, slots, channels = spec_ref.shape
     quart = channels // 4
     half = 2 * lats * quart
-    step = pl.program_id(0)
-    nsteps = pl.num_programs(0)
-
-    @pl.when(step == 0)
-    def _():
-        for j in range(blocks):
-            cols = pl.ds(j * slots, slots)
-            even = even_ref[pl.ds(0, 1), cols]
-            for k in range(lats):
-                turned = lax.dot_general(
-                    pick_ref[...], spec_ref[j, k], (((1,), (1,)), ((), ())),
-                    preferred_element_type=F32,
-                )
-                evens = turned * even
-                odds = turned - evens
-                for o, part in enumerate((evens, odds)):
-                    part = part.astype(BF16)
-                    for h in range(2):
-                        rows = pl.ds(o * half + (h * lats + k) * quart, quart)
-                        left_cos[rows, cols] = part[h * quart:(h + 1) * quart]
-                        left_sin[rows, cols] = part[(2 + h) * quart:(3 + h) * quart]
-
-    cosines = jnp.dot(left_cos[...], cos_ref[...], preferred_element_type=F32)
-    sines = jnp.dot(left_sin[...], sin_ref[...], preferred_element_type=F32)
-    cos_sum = cosines[:half] + cosines[half:]
-    cos_dif = cosines[:half] - cosines[half:]
-    sin_sum = sines[:half] + sines[half:]
-    sin_dif = sines[:half] - sines[half:]
+    for copy in copies[0] + copies[1]:
+        copy.start()
     pairs = half // 2
-    width = cos_ref.shape[1]
-    cols = pl.ds(pl.multiple_of(step * width, width), width)
+    for j in range(blocks):
+        cols = pl.ds(j * slots, slots)
+        even = even_ref[pl.ds(0, 1), cols]
+        for k in range(lats):
+            turned = lax.dot_general(
+                pick_ref[...], spec_ref[j, k], (((1,), (1,)), ((), ())),
+                preferred_element_type=F32,
+            )
+            evens = turned * even
+            odds = turned - evens
+            for o, part in enumerate((evens, odds)):
+                part = part.astype(BF16)
+                for h in range(2):
+                    rows = pl.ds(o * half + (h * lats + k) * quart, quart)
+                    left_cos[rows, cols] = part[h * quart:(h + 1) * quart]
+                    left_sin[rows, cols] = part[(2 + h) * quart:(3 + h) * quart]
 
     def product(grid):
         return (grid[:pairs] * grid[pairs:]).astype(BF16)
 
-    plus[:, cols] = product(cos_sum - sin_sum)
-    minus[:, cols] = product(cos_dif - sin_dif)
-
-    @pl.when(step < nsteps - 1)
-    def _():
-        first = product(cos_sum + sin_sum).reshape(lats, quart, width)
-        third = product(cos_dif + sin_dif).reshape(lats, quart, width)
-        out_ref[:, :, cols] = first
-        out_ref[:, :, pl.ds(pl.multiple_of(2 * QUARTER + step * width, width), width)] = third
-
-    @pl.when(step == nsteps - 1)
-    def _():
-        for b in range(QUARTER // 128):
-            source = pl.ds(QUARTER - 128 - 128 * b, 256)
-            for start, held in ((3 * QUARTER, plus), (QUARTER, minus)):
-                block = jnp.dot(held[:, source], turn_ref[...], preferred_element_type=F32)
-                out_ref[:, :, pl.ds(start + 128 * b, 128)] = block.astype(BF16).reshape(
-                    lats, quart, 128
-                )
+    for start in range(0, WIDE, BLOCK):
+        cols = pl.ds(start, BLOCK)
+        at = start // BLOCK
+        for copy in copies[at]:
+            copy.wait()
+        if at + 2 < len(copies):
+            for copy in copies[at + 2]:
+                copy.start()
+        cosines = jnp.dot(left_cos[...], cos_ref[at], preferred_element_type=F32)
+        sines = jnp.dot(left_sin[...], sin_ref[at], preferred_element_type=F32)
+        cos_sum = cosines[:half] + cosines[half:]
+        cos_dif = cosines[:half] - cosines[half:]
+        sin_sum = sines[:half] + sines[half:]
+        sin_dif = sines[:half] - sines[half:]
+        plus[:, cols] = product(cos_sum - sin_sum)
+        minus[:, cols] = product(cos_dif - sin_dif)
+        if start < QUARTER:
+            first = product(cos_sum + sin_sum).reshape(lats, quart, BLOCK)
+            third = product(cos_dif + sin_dif).reshape(lats, quart, BLOCK)
+            out_ref[:, :, cols] = first
+            out_ref[:, :, pl.ds(2 * QUARTER + start, BLOCK)] = third
+
+    for b in range(QUARTER // 128):
+        source = pl.ds(QUARTER - 128 - 128 * b, 256)
+        for start, held in ((3 * QUARTER, plus), (QUARTER, minus)):
+            block = jnp.dot(held[:, source], turn_ref[...], preferred_element_type=F32)
+            out_ref[:, :, pl.ds(start + 128 * b, 128)] = block.astype(BF16).reshape(
+                lats, quart, 128
+            )
 
 
 def fourier_products(spectra, order_table, cos_table, sin_table):
@@ -263,27 +309,20 @@
     place = part * fields + (field % 2) * (fields // 2) + field // 2
     pick = (lax.iota(jnp.int32, channels)[:, None] == place[None, :]).astype(BF16)
     turn = (lax.iota(jnp.int32, 256)[:, None] == 128 - lax.iota(jnp.int32, 128)[None, :]).astype(BF16)
-    width = 256
-    full = lambda shape: pl.BlockSpec(shape, lambda i: (0,) * len(shape))
     half = lats * fields
     return pl.pallas_call(
         fourier_kernel,
         out_shape=jax.ShapeDtypeStruct((lats, fields // 2, NLON), BF16),
-        grid=(WIDE // width,),
-        in_specs=[
-            full(spectra.shape),
-            full(even.shape),
-            full(pick.shape),
-            full(turn.shape),
-            pl.BlockSpec((count, width), lambda i: (0, i)),
-            pl.BlockSpec((count, width), lambda i: (0, i)),
-        ],
-        out_specs=full((lats, fields // 2, NLON)),
+        in_specs=[pl.BlockSpec(memory_space=pltpu.VMEM)] * 4 + [pl.BlockSpec(memory_space=pl.ANY)] * 2,
         scratch_shapes=[
             pltpu.VMEM((2 * half, count), BF16),
             pltpu.VMEM((2 * half, count), BF16),
             pltpu.VMEM((half // 2, WIDE), BF16),
             pltpu.VMEM((half // 2, WIDE), BF16),
+            pltpu.VMEM((WIDE // BLOCK, count, BLOCK), BF16),
+            pltpu.VMEM((WIDE // BLOCK, count, BLOCK), BF16),
+            pltpu.SemaphoreType.DMA((WIDE // BLOCK,)),
+            pltpu.SemaphoreType.DMA((WIDE // BLOCK,)),
         ],
         compiler_params=pltpu.CompilerParams(vmem_limit_bytes=40 * 2**20),
         name="fourier_products",
@@ -328,7 +367,9 @@
         state[k, way], after = pass_sums(state[k, way], units[way][0], after, before)
     ends = []
     for way in range(2):
-        end, after = turn_sums([state[k, way] for k in range(len(CHUNKS))], units[way][1], after)
+        second_phase = turn_sums if way == 0 else halve_sums
+        held = [state[k, way] for k in range(len(CHUNKS))]
+        end, after = second_phase(held, units[way][1], after)
         ends.append(end)
     pair = ends[0] + ends[1]
     rows = pair[0].shape[0]

time: 146 us -> 143 us (0.979)
  starting transfers between devices: 41.9 us -> 39.3 us
  Pallas kernels: 42.5 us -> 40.3 us
    ppermute x22 -> x23, starting transfers between devices: 29.5 us -> 27.4 us  [exchange(): lax.ppermute(array, 'deg', [(d, d ^ bits) for d in range(SIDE * SIDE)])]
    pallas_call x1, Pallas kernels: 8.51 us -> 6.96 us  [fourier_products(): pl.pallas_call(fourier_kernel, out_shape=jax.ShapeDtypeStruct((lats, fiel...]
    ppermute x22 -> x23, waiting for transfers between devices: 41.3 us -> 42.3 us  [exchange(): lax.ppermute(array, 'deg', [(d, d ^ bits) for d in range(SIDE * SIDE)])]
    pallas_call x7 -> x8, Pallas kernels: 5.27 us -> 4.67 us  [call(): pl.pallas_call(lambda _, *refs: kernel(*refs), out_shape=[jax.ShapeDtypeS...]
  transfers between devices with their start and end apart: 23 -> 24, of which waited for: 12 -> 13; matrix products, arithmetic and copies ran while one was open for 3% -> 3% of each run, Pallas kernels for 16% -> 16%
where the time goes in v4:
time: 143 us; the launch traced here: 142 us
  waiting for transfers between devices  57.3 us (40%)
  Pallas kernels  40.3 us (28%)
  starting transfers between devices  39.3 us (27%)
  other arithmetic  4.38 us (3%)
    ppermute x23, waiting for transfers between devices, exchange(): lax.ppermute(array, 'deg', [(d, d ^ bits) for d in range(SIDE * SIDE)])  42.3 us
    ppermute x23, starting transfers between devices, exchange(): lax.ppermute(array, 'deg', [(d, d ^ bits) for d in range(SIDE * SIDE)])  27.4 us
    pallas_call x4, Pallas kernels, legendre_sums(): pl.pallas_call(functools.partial(legendre_kernel, strides=strides), out_s...  22.1 us
    all_to_all x1, waiting for transfers between devices, local(): lax.all_to_all(sent, 'ord', split_axis=0, concat_axis=0, tiled=True)  15 us
    all_to_all x1, starting transfers between devices, local(): lax.all_to_all(sent, 'ord', split_axis=0, concat_axis=0, tiled=True)  11.8 us
    pallas_call x1, Pallas kernels, fourier_products(): pl.pallas_call(fourier_kernel, out_shape=jax.ShapeDtypeStruct((lats, fiel...  6.96 us
    pallas_call x1, Pallas kernels, build_tables(): pl.pallas_call(table_kernel, out_shape=[pltpu.HBM((WIDE // BLOCK, count,...  6.61 us
    pallas_call x8, Pallas kernels, call(): pl.pallas_call(lambda _, *refs: kernel(*refs), out_shape=[jax.ShapeDtypeS...  4.67 us
  transfers between devices with their start and end apart: 24, of which 13 were waited for; matrix products, arithmetic and copies ran while one was open for 3% of the time, Pallas kernels for 16%

profile of v4, /device:TPU:1, one launch (start us, length us, event | category | flops | bytes accessed | tf_op | source)
XLA Modules:
  0.0 142.2 jit_solution(16383218335189270857)
XLA Ops:
  0.1 4.1 %legendre_sums.4 = (bf16[4,16,48,128]{3,2,1,0:T(8,128)(2,1)S(1)}, bf16[4,16,48,128]{3,2,1,0:T(8,128)(2,1)S(1)}, bf16[2,16,48,128]{3,2,1,0:T(8,128)(2,1)S(1)}, bf...) custom-call(s32[2]{0:T(128)S(1)} %get-tuple-element.118.place_ref, bf16[256,128,256]{2,1,0:T(8,128)(2,1)} %leg_ref.7, ...), custom_call_target="tpu_custom_call" | custom-call | tf_op jit(solution)/shard_map/legendre_sums/pallas_call | solution.py:56
  4.2 4.2 %legendre_sums.5 = (bf16[4,16,48,128]{3,2,1,0:T(8,128)(2,1)S(1)}, bf16[4,16,48,128]{3,2,1,0:T(8,128)(2,1)S(1)}, bf16[2,16,48,128]{3,2,1,0:T(8,128)(2,1)S(1)}, bf...) custom-call(s32[2]{0:T(128)S(1)} %get-tuple-element.117.place_ref, bf16[256,128,256]{2,1,0:T(8,128)(2,1)} %leg_ref.7, ...), custom_call_target="tpu_custom_call" | custom-call | tf_op jit(solution)/shard_map/legendre_sums/pallas_call | solution.py:56
  8.4 2.2 %collective-permute-start.2 = (bf16[4,16,48,128]{3,2,1,0:T(8,128)(2,1)S(1)}, bf16[4,16,48,128]{3,2,1,0:T(8,128)(2,1)S(1)}, u32[]{:S(2)}, u32[]{:S(2)}) collective-permute-start(bf16[4,16,48,128]{3,2,1,0:T(8,128)(2,1)S(1)} %get-tuple-element.67), channel_id=1, source_target_pairs={{0,32},{8,40},{16,48},{24,56},{32,0},{40,8},{48,16},{56,24},{64,96... | collective-permute-start | bytes 2359304 | tf_op jit(solution)/shard_map/ppermute | solution.py:155
  11.8 1.8 %collective-permute-start.1 = (bf16[4,16,48,128]{3,2,1,0:T(8,128)(2,1)S(1)}, bf16[4,16,48,128]{3,2,1,0:T(8,128)(2,1)S(1)}, u32[]{:S(2)}, u32[]{:S(2)}) collective-permute-start(bf16[4,16,48,128]{3,2,1,0:T(8,128)(2,1)S(1)} %get-tuple-element.64), channel_id=1, source_target_pairs={{0,24},{8,16},{16,8},{24,0},{32,56},{40,48},{48,40},{56,32},{64,88... | collective-permute-start | bytes 2359304 | tf_op jit(solution)/shard_map/ppermute | solution.py:155
  13.6 1.9 %collective-permute-start.3 = (bf16[4,16,48,128]{3,2,1,0:T(8,128)(2,1)S(1)}, bf16[4,16,48,128]{3,2,1,0:T(8,128)(2,1)S(1)}, u32[]{:S(2)}, u32[]{:S(2)}) collective-permute-start(bf16[4,16,48,128]{3,2,1,0:T(8,128)(2,1)S(1)} %get-tuple-element.68), channel_id=1, source_target_pairs={{0,96},{8,104},{16,112},{24,120},{32,64},{40,72},{48,80},{56,88},{... | collective-permute-start | bytes 2359304 | tf_op jit(solution)/shard_map/ppermute | solution.py:155
  15.5 6.9 %legendre_sums.6 = (bf16[4,16,80,128]{3,2,1,0:T(8,128)(2,1)}, bf16[4,16,80,128]{3,2,1,0:T(8,128)(2,1)S(1)}, bf16[2,16,80,128]{3,2,1,0:T(8,128)(2,1)S(1)}, bf16[2...) custom-call(s32[2]{0:T(128)S(1)} %get-tuple-element.118.place_ref, bf16[256,128,256]{2,1,0:T(8,128)(2,1)} %leg_ref.7, ...), custom_call_target="tpu_custom_call" | custom-call | tf_op jit(solution)/shard_map/legendre_sums/pallas_call | solution.py:56
  22.4 6.9 %legendre_sums.7 = (bf16[4,16,80,128]{3,2,1,0:T(8,128)(2,1)}, bf16[4,16,80,128]{3,2,1,0:T(8,128)(2,1)S(1)}, bf16[2,16,80,128]{3,2,1,0:T(8,128)(2,1)S(1)}, bf16[2...) custom-call(s32[2]{0:T(128)S(1)} %get-tuple-element.117.place_ref, bf16[256,128,256]{2,1,0:T(8,128)(2,1)} %leg_ref.7, ...), custom_call_target="tpu_custom_call" | custom-call | tf_op jit(solution)/shard_map/legendre_sums/pallas_call | solution.py:56
  30.8 1.8 %collective-permute-start.5 = (bf16[4,16,80,128]{3,2,1,0:T(8,128)(2,1)S(1)}, bf16[4,16,80,128]{3,2,1,0:T(8,128)(2,1)S(1)}, u32[]{:S(2)}, u32[]{:S(2)}) collective-permute-start(bf16[4,16,80,128]{3,2,1,0:T(8,128)(2,1)S(1)} %get-tuple-element.74), channel_id=1, source_target_pairs={{0,24},{8,16},{16,8},{24,0},{32,56},{40,48},{48,40},{56,32},{64,88... | collective-permute-start | bytes 3932168 | tf_op jit(solution)/shard_map/ppermute | solution.py:155
  32.6 1.9 %collective-permute-start.7 = (bf16[4,16,80,128]{3,2,1,0:T(8,128)(2,1)S(1)}, bf16[4,16,80,128]{3,2,1,0:T(8,128)(2,1)S(1)}, u32[]{:S(2)}, u32[]{:S(2)}) collective-permute-start(bf16[4,16,80,128]{3,2,1,0:T(8,128)(2,1)S(1)} %get-tuple-element.80), channel_id=1, source_target_pairs={{0,96},{8,104},{16,112},{24,120},{32,64},{40,72},{48,80},{56,88},{... | collective-permute-start | bytes 3932168 | tf_op jit(solution)/shard_map/ppermute | solution.py:155
  34.6 4.2 %sine_multiply_fusion = (f32[2048,128]{1,0:T(8,128)S(1)}, f32[2048,128]{1,0:T(8,128)S(1)}) fusion(s32[2048]{0:T(1024)S(1)} %copy-done, f32[2048]{0:T(1024)S(1)} %get-tuple-element.116), kind=kLoop, calls=%fused_computation.6 | loop fusion | flops 4194304 | bytes 2113536 | tf_op jit(solution)/shard_map/mul | solution.py:233
  39.5 6.6 %build_tables.1 = (bf16[5,2048,256]{2,1,0:T(8,128)(2,1)}, bf16[5,2048,256]{2,1,0:T(8,128)(2,1)}) custom-call(bf16[2,16,80,128]{3,2,1,0:T(8,128)(2,1)S(1)} %get-tuple-element.61._.refs_3_, f32[2048,128]{1,0:T(8,128)S(1)} %get-tuple-element.112.cos_ref, f32[2048,128]{1,0:T(8,128)S(1)} %get-tuple-element.111.sin_ref, ...), custom_call_target="tpu_custom_call" | custom-call | tf_op jit(solution)/shard_map/build_tables/pallas_call | solution.py:225
  47.1 10.9 %collective-permute-done.6.refs_0_.refs_5_ = bf16[4,16,80,128]{3,2,1,0:T(8,128)(2,1)S(1)} collective-permute-done((bf16[4,16,80,128]{3,2,1,0:T(8,128)(2,1)}, bf16[4,16,80,128]{3,2,1,0:T(8,128)(2,1)S(1)}, u32[]{:S(2)}, u32[]{:S(2)}) %collective-permute-start.6) | collective-permute-done | bytes 1310752 | tf_op jit(solution)/shard_map/ppermute | solution.py:155
  61.9 1.9 %collective-permute-start.12 = (bf16[2,16,48,128]{3,2,1,0:T(8,128)(2,1)S(1)}, bf16[2,16,48,128]{3,2,1,0:T(8,128)(2,1)S(1)}, u32[]{:S(2)}, u32[]{:S(2)}) collective-permute-start(bf16[2,16,48,128]{3,2,1,0:T(8,128)(2,1)S(1)} %get-tuple-element.93), channel_id=1, source_target_pairs={{0,96},{8,104},{16,112},{24,120},{32,64},{40,72},{48,80},{56,88},{... | collective-permute-start | bytes 1179656 | tf_op jit(solution)/shard_map/ppermute | solution.py:155
  67.1 2.0 %collective-permute-done.8.refs_2_ = bf16[2,16,48,128]{3,2,1,0:T(8,128)(2,1)S(1)} collective-permute-done((bf16[2,16,48,128]{3,2,1,0:T(8,128)(2,1)}, bf16[2,16,48,128]{3,2,1,0:T(8,128)(2,1)S(1)}, u32[]{:S(2)}, u32[]{:S(2)}) %collective-permute-start.8) | collective-permute-done | bytes 393248 | tf_op jit(solution)/shard_map/ppermute | solution.py:155
  70.9 1.9 %collective-permute-start.14 = (bf16[2,16,80,128]{3,2,1,0:T(8,128)(2,1)S(1)}, bf16[2,16,80,128]{3,2,1,0:T(8,128)(2,1)S(1)}, u32[]{:S(2)}, u32[]{:S(2)}) collective-permute-start(bf16[2,16,80,128]{3,2,1,0:T(8,128)(2,1)S(1)} %get-tuple-element.97), channel_id=1, source_target_pairs={{0,96},{8,104},{16,112},{24,120},{32,64},{40,72},{48,80},{56,88},{... | collective-permute-start | bytes 1966088 | tf_op jit(solution)/shard_map/ppermute | solution.py:155
  72.8 6.4 %collective-permute-done.11.refs_8_ = bf16[2,16,80,128]{3,2,1,0:T(8,128)(2,1)S(1)} collective-permute-done((bf16[2,16,80,128]{3,2,1,0:T(8,128)(2,1)S(1)}, bf16[2,16,80,128]{3,2,1,0:T(8,128)(2,1)S(1)}, u32[]{:S(2)}, u32[]{:S(2)}) %collective-permute-start.11) | collective-permute-done | bytes 655392 | tf_op jit(solution)/shard_map/ppermute | solution.py:155
  79.2 3.3 %collective-permute-done.10.refs_7_ = bf16[2,16,80,128]{3,2,1,0:T(8,128)(2,1)S(1)} collective-permute-done((bf16[2,16,80,128]{3,2,1,0:T(8,128)(2,1)S(1)}, bf16[2,16,80,128]{3,2,1,0:T(8,128)(2,1)S(1)}, u32[]{:S(2)}, u32[]{:S(2)}) %collective-permute-start.10) | collective-permute-done | bytes 655392 | tf_op jit(solution)/shard_map/ppermute | solution.py:155
  86.2 2.8 %collective-permute-start.19 = (bf16[16,128,128]{2,1,0:T(8,128)(2,1)S(1)}, bf16[16,128,128]{2,1,0:T(8,128)(2,1)S(1)}, u32[]{:S(2)}, u32[]{:S(2)}) collective-permute-start(bf16[16,128,128]{2,1,0:T(8,128)(2,1)S(1)} %get-tuple-element.106), channel_id=1, source_target_pairs={{0,96},{8,104},{16,112},{24,120},{32,64},{40,72},{48,80},{56,88},{... | collective-permute-start | bytes 1572872 | tf_op jit(solution)/shard_map/ppermute | solution.py:155
  89.3 3.6 %collective-permute-done.16.refs_0_.refs_4_ = bf16[16,128,128]{2,1,0:T(8,128)(2,1)S(1)} collective-permute-done((bf16[16,128,128]{2,1,0:T(8,128)(2,1)S(1)}, bf16[16,128,128]{2,1,0:T(8,128)(2,1)S(1)}, u32[]{:S(2)}, u32[]{:S(2)}) %collective-permute-start.16) | collective-permute-done | bytes 524320 | tf_op jit(solution)/shard_map/ppermute | solution.py:155
  95.9 2.2 %collective-permute-done.19.refs_2_ = bf16[16,128,128]{2,1,0:T(8,128)(2,1)S(1)} collective-permute-done((bf16[16,128,128]{2,1,0:T(8,128)(2,1)S(1)}, bf16[16,128,128]{2,1,0:T(8,128)(2,1)S(1)}, u32[]{:S(2)}, u32[]{:S(2)}) %collective-permute-start.19) | collective-permute-done | bytes 524320 | tf_op jit(solution)/shard_map/ppermute | solution.py:155
  98.0 8.6 %collective-permute-done.20.refs_3_ = bf16[16,128,128]{2,1,0:T(8,128)(2,1)S(1)} collective-permute-done((bf16[16,128,128]{2,1,0:T(8,128)(2,1)S(1)}, bf16[16,128,128]{2,1,0:T(8,128)(2,1)S(1)}, u32[]{:S(2)}, u32[]{:S(2)}) %collective-permute-start.20) | collective-permute-done | bytes 524320 | tf_op jit(solution)/shard_map/ppermute | solution.py:155
  108.1 11.8 %all-to-all-start = ((bf16[8,2,256,128]{3,2,1,0:T(8,128)(2,1)}), bf16[8,2,256,128]{3,2,1,0:T(8,128)(2,1)S(1)}, u32[]{:S(2)}, u32[]{:S(2)}) async-start(bf16[8,2,256,128]{3,2,1,0:T(8,128)(2,1)} %bitcast.2), calls=%async_computation | async-start | bytes 2097152 | tf_op jit(solution)/shard_map/all_to_all | solution.py:378
  120.0 15.0 %all-to-all-done.spec_ref = bf16[8,2,256,128]{3,2,1,0:T(8,128)(2,1)S(1)} async-done(((bf16[8,2,256,128]{3,2,1,0:T(8,128)(2,1)}), bf16[8,2,256,128]{3,2,1,0:T(8,128)(2,1)S(1)}, u32[]{:S(2)}, u32[]{:S(2)}) %all-to-all-start) | async-done | bytes 1048608 | tf_op jit(solution)/shard_map/all_to_all | solution.py:378
  135.1 7.0 %fourier_products.1 = bf16[2,32,4096]{2,1,0:T(8,128)(2,1)} custom-call(bf16[8,2,256,128]{3,2,1,0:T(8,128)(2,1)S(1)} %all-to-all-done.spec_ref, f32[8,2048]{1,0:T(8,128)S(1)} %broadcast_in_dim.42.even_ref, bf16[128,128]{1,0:T(8,128)(2,1)S(1)} %fusion.7.pick_ref, bf16[256,128]{1,0:T(8,128)(2,1)S(1)} %fusion.6.turn_ref, ...), custom_call_target="tpu_custom_call" | custom-call | tf_op jit(solution)/shard_map/fourier_products/pallas_call | solution.py:313
  (50 shorter events, 21.9 us)
Async XLA Ops:
  8.4 21.0 %collective-permute-start.2 = (bf16[4,16,48,128]{3,2,1,0:T(8,128)(2,1)S(1)}, bf16[4,16,48,128]{3,2,1,0:T(8,128)(2,1)S(1)}, u32[]{:S(2)}, u32[]{:S(2)}) collective-permute-start(bf16[4,16,48,128]{3,2,1,0:T(8,128)(2,1)S(1)} %get-tuple-element.67), channel_id=1, source_target_pairs={{0,32},{8,40},{16,48},{24,56},{32,0},{40,8},{48,16},{56,24},{64,96... | collective-permute-start | bytes 2359304 | tf_op jit(solution)/shard_map/ppermute | solution.py:155
  10.6 19.1 %collective-permute-start = (bf16[4,16,48,128]{3,2,1,0:T(8,128)(2,1)S(1)}, bf16[4,16,48,128]{3,2,1,0:T(8,128)(2,1)S(1)}, u32[]{:S(2)}, u32[]{:S(2)}) collective-permute-start(bf16[4,16,48,128]{3,2,1,0:T(8,128)(2,1)S(1)} %get-tuple-element.63), channel_id=1, source_target_pairs={{0,8},{8,0},{16,24},{24,16},{32,40},{40,32},{48,56},{56,48},{64,72... | collective-permute-start | bytes 2359304 | tf_op jit(solution)/shard_map/ppermute | solution.py:155
  11.8 19.0 %collective-permute-start.1 = (bf16[4,16,48,128]{3,2,1,0:T(8,128)(2,1)S(1)}, bf16[4,16,48,128]{3,2,1,0:T(8,128)(2,1)S(1)}, u32[]{:S(2)}, u32[]{:S(2)}) collective-permute-start(bf16[4,16,48,128]{3,2,1,0:T(8,128)(2,1)S(1)} %get-tuple-element.64), channel_id=1, source_target_pairs={{0,24},{8,16},{16,8},{24,0},{32,56},{40,48},{48,40},{56,32},{64,88... | collective-permute-start | bytes 2359304 | tf_op jit(solution)/shard_map/ppermute | solution.py:155
  13.6 19.0 %collective-permute-start.3 = (bf16[4,16,48,128]{3,2,1,0:T(8,128)(2,1)S(1)}, bf16[4,16,48,128]{3,2,1,0:T(8,128)(2,1)S(1)}, u32[]{:S(2)}, u32[]{:S(2)}) collective-permute-start(bf16[4,16,48,128]{3,2,1,0:T(8,128)(2,1)S(1)} %get-tuple-element.68), channel_id=1, source_target_pairs={{0,96},{8,104},{16,112},{24,120},{32,64},{40,72},{48,80},{56,88},{... | collective-permute-start | bytes 2359304 | tf_op jit(solution)/shard_map/ppermute | solution.py:155
  29.3 28.7 %collective-permute-start.6 = (bf16[4,16,80,128]{3,2,1,0:T(8,128)(2,1)}, bf16[4,16,80,128]{3,2,1,0:T(8,128)(2,1)S(1)}, u32[]{:S(2)}, u32[]{:S(2)}) collective-permute-start(bf16[4,16,80,128]{3,2,1,0:T(8,128)(2,1)} %get-tuple-element.78), channel_id=1, source_target_pairs={{0,32},{8,40},{16,48},{24,56},{32,0},{40,8},{48,16},{56,24},{64,96... | collective-permute-start | bytes 3932168 | tf_op jit(solution)/shard_map/ppermute | solution.py:155
  29.7 28.7 %collective-permute-start.4 = (bf16[4,16,80,128]{3,2,1,0:T(8,128)(2,1)}, bf16[4,16,80,128]{3,2,1,0:T(8,128)(2,1)S(1)}, u32[]{:S(2)}, u32[]{:S(2)}) collective-permute-start(bf16[4,16,80,128]{3,2,1,0:T(8,128)(2,1)} %get-tuple-element.72), channel_id=1, source_target_pairs={{0,8},{8,0},{16,24},{24,16},{32,40},{40,32},{48,56},{56,48},{64,72... | collective-permute-start | bytes 3932168 | tf_op jit(solution)/shard_map/ppermute | solution.py:155
  30.8 29.3 %collective-permute-start.5 = (bf16[4,16,80,128]{3,2,1,0:T(8,128)(2,1)S(1)}, bf16[4,16,80,128]{3,2,1,0:T(8,128)(2,1)S(1)}, u32[]{:S(2)}, u32[]{:S(2)}) collective-permute-start(bf16[4,16,80,128]{3,2,1,0:T(8,128)(2,1)S(1)} %get-tuple-element.74), channel_id=1, source_target_pairs={{0,24},{8,16},{16,8},{24,0},{32,56},{40,48},{48,40},{56,32},{64,88... | collective-permute-start | bytes 3932168 | tf_op jit(solution)/shard_map/ppermute | solution.py:155
  32.6 29.3 %collective-permute-start.7 = (bf16[4,16,80,128]{3,2,1,0:T(8,128)(2,1)S(1)}, bf16[4,16,80,128]{3,2,1,0:T(8,128)(2,1)S(1)}, u32[]{:S(2)}, u32[]{:S(2)}) collective-permute-start(bf16[4,16,80,128]{3,2,1,0:T(8,128)(2,1)S(1)} %get-tuple-element.80), channel_id=1, source_target_pairs={{0,96},{8,104},{16,112},{24,120},{32,64},{40,72},{48,80},{56,88},{... | collective-permute-start | bytes 3932168 | tf_op jit(solution)/shard_map/ppermute | solution.py:155
  58.0 7.9 %collective-permute-start.13 = (bf16[2,16,48,128]{3,2,1,0:T(8,128)(2,1)S(1)}, bf16[2,16,48,128]{3,2,1,0:T(8,128)(2,1)S(1)}, u32[]{:S(2)}, u32[]{:S(2)}) collective-permute-start(bf16[2,16,48,128]{3,2,1,0:T(8,128)(2,1)S(1)} %get-tuple-element.94._), channel_id=1, source_target_pairs={{0,32},{8,40},{16,48},{24,56},{32,0},{40,8},{48,16},{56,24},{64,96... | collective-permute-start | bytes 1179656 | tf_op jit(solution)/shard_map/ppermute | solution.py:155
  58.4 7.9 %collective-permute-start.9 = (bf16[2,16,48,128]{3,2,1,0:T(8,128)(2,1)S(1)}, bf16[2,16,48,128]{3,2,1,0:T(8,128)(2,1)S(1)}, u32[]{:S(2)}, u32[]{:S(2)}) collective-permute-start(bf16[2,16,48,128]{3,2,1,0:T(8,128)(2,1)S(1)} %get-tuple-element.85._), channel_id=1, source_target_pairs={{0,8},{8,0},{16,24},{24,16},{32,40},{40,32},{48,56},{56,48},{64,72... | collective-permute-start | bytes 1179656 | tf_op jit(solution)/shard_map/ppermute | solution.py:155
  60.1 9.0 %collective-permute-start.8 = (bf16[2,16,48,128]{3,2,1,0:T(8,128)(2,1)}, bf16[2,16,48,128]{3,2,1,0:T(8,128)(2,1)S(1)}, u32[]{:S(2)}, u32[]{:S(2)}) collective-permute-start(bf16[2,16,48,128]{3,2,1,0:T(8,128)(2,1)} %get-tuple-element.84), channel_id=1, source_target_pairs={{0,24},{8,16},{16,8},{24,0},{32,56},{40,48},{48,40},{56,32},{64,88... | collective-permute-start | bytes 1179656 | tf_op jit(solution)/shard_map/ppermute | solution.py:155
  61.9 9.0 %collective-permute-start.12 = (bf16[2,16,48,128]{3,2,1,0:T(8,128)(2,1)S(1)}, bf16[2,16,48,128]{3,2,1,0:T(8,128)(2,1)S(1)}, u32[]{:S(2)}, u32[]{:S(2)}) collective-permute-start(bf16[2,16,48,128]{3,2,1,0:T(8,128)(2,1)S(1)} %get-tuple-element.93), channel_id=1, source_target_pairs={{0,96},{8,104},{16,112},{24,120},{32,64},{40,72},{48,80},{56,88},{... | collective-permute-start | bytes 1179656 | tf_op jit(solution)/shard_map/ppermute | solution.py:155
  65.9 17.4 %collective-permute-start.15 = (bf16[2,16,80,128]{3,2,1,0:T(8,128)(2,1)S(1)}, bf16[2,16,80,128]{3,2,1,0:T(8,128)(2,1)S(1)}, u32[]{:S(2)}, u32[]{:S(2)}) collective-permute-start(bf16[2,16,80,128]{3,2,1,0:T(8,128)(2,1)S(1)} %get-tuple-element.98._), channel_id=1, source_target_pairs={{0,32},{8,40},{16,48},{24,56},{32,0},{40,8},{48,16},{56,24},{64,96... | collective-permute-start | bytes 1966088 | tf_op jit(solution)/shard_map/ppermute | solution.py:155
  66.3 12.9 %collective-permute-start.11 = (bf16[2,16,80,128]{3,2,1,0:T(8,128)(2,1)S(1)}, bf16[2,16,80,128]{3,2,1,0:T(8,128)(2,1)S(1)}, u32[]{:S(2)}, u32[]{:S(2)}) collective-permute-start(bf16[2,16,80,128]{3,2,1,0:T(8,128)(2,1)S(1)} %get-tuple-element.89._), channel_id=1, source_target_pairs={{0,8},{8,0},{16,24},{24,16},{32,40},{40,32},{48,56},{56,48},{64,72... | collective-permute-start | bytes 1966088 | tf_op jit(solution)/shard_map/ppermute | solution.py:155
  69.1 13.4 %collective-permute-start.10 = (bf16[2,16,80,128]{3,2,1,0:T(8,128)(2,1)S(1)}, bf16[2,16,80,128]{3,2,1,0:T(8,128)(2,1)S(1)}, u32[]{:S(2)}, u32[]{:S(2)}) collective-permute-start(bf16[2,16,80,128]{3,2,1,0:T(8,128)(2,1)S(1)} %get-tuple-element.88), channel_id=1, source_target_pairs={{0,24},{8,16},{16,8},{24,0},{32,56},{40,48},{48,40},{56,32},{64,88... | collective-permute-start | bytes 1966088 | tf_op jit(solution)/shard_map/ppermute | solution.py:155
  70.9 13.2 %collective-permute-start.14 = (bf16[2,16,80,128]{3,2,1,0:T(8,128)(2,1)S(1)}, bf16[2,16,80,128]{3,2,1,0:T(8,128)(2,1)S(1)}, u32[]{:S(2)}, u32[]{:S(2)}) collective-permute-start(bf16[2,16,80,128]{3,2,1,0:T(8,128)(2,1)S(1)} %get-tuple-element.97), channel_id=1, source_target_pairs={{0,96},{8,104},{16,112},{24,120},{32,64},{40,72},{48,80},{56,88},{... | collective-permute-start | bytes 1966088 | tf_op jit(solution)/shard_map/ppermute | solution.py:155
  84.8 8.1 %collective-permute-start.16 = (bf16[16,128,128]{2,1,0:T(8,128)(2,1)S(1)}, bf16[16,128,128]{2,1,0:T(8,128)(2,1)S(1)}, u32[]{:S(2)}, u32[]{:S(2)}) collective-permute-start(bf16[16,128,128]{2,1,0:T(8,128)(2,1)S(1)} %get-tuple-element.101), channel_id=1, source_target_pairs={{0,8},{8,0},{16,24},{24,16},{32,40},{40,32},{48,56},{56,48},{64,72... | collective-permute-start | bytes 1572872 | tf_op jit(solution)/shard_map/ppermute | solution.py:155
  84.9 9.3 %collective-permute-start.17 = (bf16[16,128,128]{2,1,0:T(8,128)(2,1)S(1)}, bf16[16,128,128]{2,1,0:T(8,128)(2,1)S(1)}, u32[]{:S(2)}, u32[]{:S(2)}) collective-permute-start(bf16[16,128,128]{2,1,0:T(8,128)(2,1)S(1)} %get-tuple-element.102), channel_id=1, source_target_pairs={{0,24},{8,16},{16,8},{24,0},{32,56},{40,48},{48,40},{56,32},{64,88... | collective-permute-start | bytes 1572872 | tf_op jit(solution)/shard_map/ppermute | solution.py:155
  86.0 9.8 %collective-permute-start.18 = (bf16[16,128,128]{2,1,0:T(8,128)(2,1)S(1)}, bf16[16,128,128]{2,1,0:T(8,128)(2,1)S(1)}, u32[]{:S(2)}, u32[]{:S(2)}) collective-permute-start(bf16[16,128,128]{2,1,0:T(8,128)(2,1)S(1)} %get-tuple-element.105), channel_id=1, source_target_pairs={{0,32},{8,40},{16,48},{24,56},{32,0},{40,8},{48,16},{56,24},{64,96... | collective-permute-start | bytes 1572872 | tf_op jit(solution)/shard_map/ppermute | solution.py:155
  86.2 11.9 %collective-permute-start.19 = (bf16[16,128,128]{2,1,0:T(8,128)(2,1)S(1)}, bf16[16,128,128]{2,1,0:T(8,128)(2,1)S(1)}, u32[]{:S(2)}, u32[]{:S(2)}) collective-permute-start(bf16[16,128,128]{2,1,0:T(8,128)(2,1)S(1)} %get-tuple-element.106), channel_id=1, source_target_pairs={{0,96},{8,104},{16,112},{24,120},{32,64},{40,72},{48,80},{56,88},{... | collective-permute-start | bytes 1572872 | tf_op jit(solution)/shard_map/ppermute | solution.py:155
  89.0 17.7 %collective-permute-start.20 = (bf16[16,128,128]{2,1,0:T(8,128)(2,1)S(1)}, bf16[16,128,128]{2,1,0:T(8,128)(2,1)S(1)}, u32[]{:S(2)}, u32[]{:S(2)}) collective-permute-start(bf16[16,128,128]{2,1,0:T(8,128)(2,1)S(1)} %get-tuple-element.107), channel_id=1, source_target_pairs={{0,64},{8,72},{16,80},{24,88},{32,96},{40,104},{48,112},{56,120},{... | collective-permute-start | bytes 1572872 | tf_op jit(solution)/shard_map/ppermute | solution.py:155
  94.3 12.4 %collective-permute-start.21 = (bf16[8,128,128]{2,1,0:T(8,128)(2,1)S(1)}, bf16[8,128,128]{2,1,0:T(8,128)(2,1)S(1)}, u32[]{:S(2)}, u32[]{:S(2)}) collective-permute-start(bf16[8,128,128]{2,1,0:T(8,128)(2,1)S(1)} %get-tuple-element.108), channel_id=1, source_target_pairs={{0,24},{8,16},{16,8},{24,0},{32,56},{40,48},{48,40},{56,32},{64,88... | collective-permute-start | bytes 786440 | tf_op jit(solution)/shard_map/ppermute | solution.py:155
  95.8 10.8 %collective-permute-start.22 = (bf16[8,128,128]{2,1,0:T(8,128)(2,1)S(1)}, bf16[8,128,128]{2,1,0:T(8,128)(2,1)S(1)}, u32[]{:S(2)}, u32[]{:S(2)}) collective-permute-start(bf16[8,128,128]{2,1,0:T(8,128)(2,1)S(1)} %get-tuple-element.104._), channel_id=1, source_target_pairs={{0,8},{8,0},{16,24},{24,16},{32,40},{40,32},{48,56},{56,48},{64,72... | collective-permute-start | bytes 786440 | tf_op jit(solution)/shard_map/ppermute | solution.py:155
  108.1 26.9 %all-to-all-start = ((bf16[8,2,256,128]{3,2,1,0:T(8,128)(2,1)}), bf16[8,2,256,128]{3,2,1,0:T(8,128)(2,1)S(1)}, u32[]{:S(2)}, u32[]{:S(2)}) async-start(bf16[8,2,256,128]{3,2,1,0:T(8,128)(2,1)} %bitcast.2), calls=%async_computation | async-start | bytes 2097152 | tf_op jit(solution)/shard_map/all_to_all | solution.py:378
  (1 other events, 12.1 us)
